TPU v7x, 128 devices: a whole 4x4x4 slice. The times are simulated.
128 devices in a mesh: order: 4 (over z), shard: 32 (over x, y, core).
Axes of the slice: x: 4, y: 4, z: 4, core: 2. Of those that a mesh axis runs over, the one named last changes fastest.
Arguments:
- sky_coeffs: float32 [32, 2, 2048], P('shard'), may hold values from -6 to 6
- beam_coeffs: float32 [64, 2048], P('order'), may hold values from -0.09375 to 0.09375
- wigner: bfloat16 [32, 64, 2048, 128], P('shard', 'order'), may hold values from -0.125 to 0.125
- visits: int32 [128, 128, 4], P(('order', 'shard')), may hold values from -1 to 127, as said below
- point_slot: int32 [2097152], P(('order', 'shard')), may hold values from 0 to 511, as said below
- phi_cell: int32 [2097152], P(('order', 'shard')), may hold values from 0 to 30
- psi_cell: int32 [2097152], P(('order', 'shard')), may hold values from 0 to 127
- fraction: float32 [2, 2097152], P(None, ('order', 'shard')), may hold values from 0 to 1
Outputs:
- timeline: float32 [2097152], P(('order', 'shard'))
Inputs may be any that keep to these rules, and one draw needn't show every extreme that they name: Live entries of one row visits[r, d] are distinct tiles of owner d and come first; every row holds 1 to 4 live entries; for every device r some owner d has all 4 entries live. `point_slot`: every pointing names a live entry of its own device's visit list. Of one device's pointings, exactly 192 name each of half of the owners and 64 each of the others.
All inputs are finite; a program needn't handle non-finite values.
Results may differ from a plain program's by a relative error of at most 0.008.
Values may be sent and summed in bfloat16 or wider, within the bound.
No kernel may reach another device: no remote copies, remote signals or barrier semaphores. Data moves between devices by JAX's collectives and lax.ppermute only.
A program may use at most 64 MiB of HBM per device.

v0:
```python
import math

import jax
import jax.numpy as jnp
import numpy as np
from jax import lax
from jax.experimental import pallas as pl
from jax.experimental.pallas import tpu as pltpu
from jax.sharding import PartitionSpec as P

BF = jnp.bfloat16
F32 = jnp.float32
MESH_AXES = ("order", "shard")
NPHI = 4096
NPSI = 128
MODES = 32
ORDERS = 64
GROUPS = 4
SHARDS = 32
OWNERS = 128
LANES = 128
RANKS = 256
ITEMS = 6
NT = (((1,), (1,)), ((), ()))


def phi_tables():
    phi = np.arange(NPHI, dtype=np.int64)[:, None]
    mode = np.arange(MODES, dtype=np.int64)[None, :]
    phase = ((phi * mode) % NPHI).astype(np.float64) * (2.0 * math.pi / NPHI)
    both = np.concatenate([np.cos(phase), -np.sin(phase)], axis=1)
    blocks = both.reshape(NPHI // 32, 32, 2 * MODES).transpose(0, 2, 1)
    return np.tile(blocks, (1, 1, 4)).astype(jnp.bfloat16)


def psi_tables():
    psi = np.arange(NPSI, dtype=np.int64)[:, None]
    order = np.arange(ORDERS, dtype=np.int64)[None, :]
    phase = ((psi * order) % NPSI).astype(np.float64) * (2.0 * math.pi / NPSI)
    cos, sin = np.cos(phase), np.sin(phase)
    real = np.stack([cos, -sin], axis=2).reshape(NPSI, 2 * ORDERS)
    imag = np.stack([sin, cos], axis=2).reshape(NPSI, 2 * ORDERS)
    return np.concatenate([real, imag], axis=0).astype(jnp.bfloat16)


def bucket_kernel(slot_ref, phi_ref, psi_ref, frac_ref, g_ref, rank_ref, carry, lhs, hot):
    own_iota = lax.broadcasted_iota(jnp.int32, (OWNERS, LANES), 0)
    rank_iota = lax.broadcasted_iota(jnp.int32, (RANKS, LANES), 0)
    before = (
        lax.broadcasted_iota(jnp.int32, (LANES, 2 * LANES), 0)
        < lax.broadcasted_iota(jnp.int32, (LANES, 2 * LANES), 1)
    ).astype(F32).astype(BF)
    carry[...] = jnp.zeros_like(carry)
    g_ref[...] = jnp.zeros_like(g_ref)

    def block(step, _):
        start = pl.multiple_of(step * 8, 8)
        slots = slot_ref[pl.ds(start, 8), :]
        owners = slots >> 2
        rows = ((slots & 3) * 32 + phi_ref[pl.ds(start, 8), :]).astype(F32)
        psis = psi_ref[pl.ds(start, 8), :].astype(F32)
        a = frac_ref[0, pl.ds(start, 8), :]
        b = frac_ref[1, pl.ds(start, 8), :]
        a_hi = a.astype(BF).astype(F32)
        b_hi = b.astype(BF).astype(F32)
        items = (rows, psis, a_hi, a - a_hi, b_hi, b - b_hi)
        seen = carry[...]
        ranks = []
        for u in range(8):
            mask = own_iota == owners[u : u + 1]
            hot_own = jnp.where(mask, 1.0, 0.0).astype(BF)
            count = jnp.dot(hot_own, before, preferred_element_type=F32)
            place = count[:, :LANES] + seen
            seen = seen + count[:, LANES:]
            rank = jnp.sum(jnp.where(mask, place, 0.0), axis=0, keepdims=True)
            ranks.append(rank)
            hot[:, u * LANES : (u + 1) * LANES] = jnp.where(
                rank_iota == rank.astype(jnp.int32), 1.0, 0.0
            ).astype(BF)
            for n, item in enumerate(items):
                lhs[n * OWNERS : (n + 1) * OWNERS, u * LANES : (u + 1) * LANES] = jnp.where(
                    mask, item[u : u + 1], 0.0
                ).astype(BF)
        carry[...] = seen
        rank_ref[pl.ds(start, 8), :] = jnp.concatenate(ranks, axis=0)
        g_ref[...] += lax.dot_general(lhs[...], hot[...], NT, preferred_element_type=F32)
        return 0

    lax.fori_loop(0, 16, block, 0)


def eval_kernel(
    visits_ref, coeff_ref, w_ref, phi_ref, g_ref, slot_ref, rank_ref, out_ref, coeff, found, pair
):
    def widen(step, _):
        start = pl.multiple_of(step * 128, 128)
        coeff[pl.ds(start, 128), :] = coeff_ref[pl.ds(start, 128), :].astype(F32)
        return 0

    lax.fori_loop(0, 32, widen, 0)
    lane = lax.broadcasted_iota(jnp.int32, (1, LANES), 1) // 32
    row_iota = lax.broadcasted_iota(jnp.int32, (LANES, RANKS), 0)

    def shard(s, _):
        block = coeff[pl.ds(s, 128, stride=SHARDS), :]
        turned = [block] + [pltpu.roll(block, 32 * n, axis=1) for n in (1, 2, 3)]
        rows = []
        for row in range(4):
            part = None
            for o in range(4):
                piece = turned[(o - row) % 4][o * 32 : (o + 1) * 32]
                part = piece if part is None else jnp.where(lane == o, piece, part)
            rows.append(part)
        block = jnp.concatenate(rows, axis=0).astype(BF)
        both = lax.dot_general(w_ref[...], block, NT, preferred_element_type=F32).astype(BF)
        both = jnp.concatenate([both[:NPSI], both[NPSI:]], axis=1)
        for o in range(4):
            d = o * SHARDS + s
            waves, lane_row = None, None
            for j in range(4):
                tile = jnp.maximum(visits_ref[d * 4 + j], 0)
                wave = phi_ref[o * 32 + (tile & 31)]
                row = jnp.full((1, LANES), tile >> 5, jnp.int32)
                waves = wave if j == 0 else jnp.where(lane == j, wave, waves)
                lane_row = row if j == 0 else jnp.where(lane == j, row, lane_row)
            parts = []
            for c in range(2):
                for row in range(4):
                    parts.append(
                        jnp.where(lane_row == row, waves[c * 32 : (c + 1) * 32], jnp.zeros((), BF))
                    )
            chosen = jnp.concatenate(parts, axis=0)
            tiles = jnp.dot(both, chosen, preferred_element_type=F32).astype(BF)
            at = [g_ref[pl.ds(n * OWNERS + d, 1), :] for n in range(ITEMS)]
            row0 = at[0].astype(jnp.int32)
            q0 = at[1].astype(jnp.int32)
            q1 = (q0 + 1) & (NPSI - 1)
            a = at[2] + at[3]
            b = at[4] + at[5]
            one_a = 1.0 - a
            lo = one_a.astype(BF).astype(F32)
            hi = a.astype(BF).astype(F32)
            on0 = row_iota == row0
            on1 = row_iota == row0 + 1
            main = jnp.where(on0, lo, jnp.where(on1, hi, 0.0)).astype(BF)
            rest = jnp.where(on0, one_a - lo, jnp.where(on1, a - hi, 0.0)).astype(BF)
            seen = jnp.dot(
                jnp.concatenate([tiles, tiles], axis=1),
                jnp.concatenate([main, rest], axis=0),
                preferred_element_type=F32,
            )
            weight = jnp.where(row_iota == q0, 1.0 - b, jnp.where(row_iota == q1, b, 0.0))
            found[pl.ds(d, 1), :] = jnp.sum(seen * weight, axis=0, keepdims=True)
        return 0

    lax.fori_loop(0, SHARDS, shard, 0)

    value = found[...]
    high = value.astype(BF)
    pair[:OWNERS, :] = high
    pair[OWNERS:, :] = (value - high.astype(F32)).astype(BF)
    own_iota = lax.broadcasted_iota(jnp.int32, (OWNERS, LANES), 0)
    rank_iota = lax.broadcasted_iota(jnp.int32, (RANKS, LANES), 0)

    def back(step, _):
        start = pl.multiple_of(step * 8, 8)
        owners = slot_ref[pl.ds(start, 8), :] >> 2
        ranks = rank_ref[pl.ds(start, 8), :].astype(jnp.int32)
        result = []
        for u in range(0, 8, 2):
            hot = jnp.concatenate(
                [
                    jnp.where(rank_iota == ranks[v : v + 1], 1.0, 0.0).astype(BF)
                    for v in (u, u + 1)
                ],
                axis=1,
            )
            moved = jnp.dot(pair[...], hot, preferred_element_type=F32)
            moved = moved[:OWNERS] + moved[OWNERS:]
            for v in (u, u + 1):
                part = moved[:, (v - u) * LANES : (v - u + 1) * LANES]
                result.append(
                    jnp.sum(
                        jnp.where(own_iota == owners[v : v + 1], part, 0.0), axis=0, keepdims=True
                    )
                )
        out_ref[pl.ds(start, 8), :] = jnp.concatenate(result, axis=0)
        return 0

    lax.fori_loop(0, 16, back, 0)


def shards(sky_coeffs, beam_coeffs, wigner, visits, point_slot, phi_cell, psi_cell, fraction):
    weighted = (sky_coeffs[0][None, :, :] * beam_coeffs[:, None, :]).astype(BF)
    coeffs = jnp.einsum("kcl,klt->tkc", weighted, wigner[0], preferred_element_type=F32)
    coeffs = coeffs.astype(BF).reshape(SHARDS, LANES)
    everyone = lax.all_to_all(
        jnp.broadcast_to(coeffs[None], (OWNERS, SHARDS, LANES)), MESH_AXES, 0, 0, tiled=True
    )
    slots = point_slot.reshape(OWNERS, LANES)
    cells = phi_cell.reshape(OWNERS, LANES)
    psis = psi_cell.reshape(OWNERS, LANES)
    fractions = fraction.reshape(2, OWNERS, LANES)
    vmem = pl.BlockSpec(memory_space=pltpu.VMEM)
    grouped, ranks = pl.pallas_call(
        bucket_kernel,
        out_shape=(
            jax.ShapeDtypeStruct((ITEMS * OWNERS, RANKS), F32),
            jax.ShapeDtypeStruct((OWNERS, LANES), F32),
        ),
        in_specs=[vmem] * 4,
        out_specs=(vmem, vmem),
        scratch_shapes=[
            pltpu.VMEM((OWNERS, LANES), F32),
            pltpu.VMEM((ITEMS * OWNERS, 1024), BF),
            pltpu.VMEM((RANKS, 1024), BF),
        ],
        compiler_params=pltpu.CompilerParams(vmem_limit_bytes=24 * 1024 * 1024),
        cost_estimate=pl.CostEstimate(
            flops=8 * 1024**3, bytes_accessed=2 * 1024**2, transcendentals=0
        ),
        name="bucket",
    )(slots, cells, psis, fractions)
    timeline = pl.pallas_call(
        eval_kernel,
        out_shape=jax.ShapeDtypeStruct((OWNERS, LANES), F32),
        in_specs=[pl.BlockSpec(memory_space=pltpu.SMEM)] + [vmem] * 6,
        out_specs=vmem,
        scratch_shapes=[
            pltpu.VMEM((OWNERS * SHARDS, LANES), F32),
            pltpu.VMEM((OWNERS, RANKS), F32),
            pltpu.VMEM((2 * OWNERS, RANKS), BF),
        ],
        compiler_params=pltpu.CompilerParams(vmem_limit_bytes=32 * 1024 * 1024),
        name="evaluate",
    )(
        visits.reshape(-1),
        everyone.reshape(OWNERS * SHARDS, LANES),
        jnp.asarray(psi_tables()),
        jnp.asarray(phi_tables()),
        grouped,
        slots,
        ranks,
    )
    return timeline.reshape(-1)


def solution(mesh):
    placed = (
        P("shard", None, None),
        P("order", None),
        P("shard", "order", None, None),
        P(("order", "shard"), None, None),
        P(("order", "shard")),
        P(("order", "shard")),
        P(("order", "shard")),
        P(None, ("order", "shard")),
    )
    return jax.shard_map(
        shards, mesh=mesh, in_specs=placed, out_specs=P(("order", "shard")), check_vma=False
    )
```

profile of v0, /device:TPU:1, one launch (start us, length us, event | category | flops | bytes accessed | tf_op | source)
XLA Modules:
  0.0 71.8 jit_solution(18314042487469648299)
XLA Ops:
  0.0 0.0 copy-start.8
  0.0 0.0 copy-start.7
  0.0 0.0 copy-start.3
  0.0 0.0 copy-start.5
  0.0 0.0 copy-start.6
  0.0 4.7 %fusion.5 = bf16[128,16,2]{0,2,1:T(2,128)(2,1)S(1)} fusion(bf16[1,16,2048,128]{3,2,1,0:T(8,128)(2,1)} %param.12, f32[16,2048]{1,0:T(8,128)} %param.11, f32[2,2048]{1,0:T(2,128)} %bitcast.26), kind=kOutput, calls=%fused_computation.3 | convolution fusion | flops 16912384 | bytes 8544256 | tf_op jit(solution)/shard_map/kcl,klt->tkc/dot_general | solution.py:195
  4.7 0.5 copy.12
  5.2 0.6 broadcast_in_dim.8
  5.9 1.1 %broadcast_in_dim.9 = bf16[128,32,128]{2,1,0:T(8,128)(2,1)} broadcast(bf16[32,128]{1,0:T(8,128)(2,1)S(1)} %broadcast_in_dim.8), dimensions={1,2} | broadcast | bytes 1056768 | tf_op jit(solution)/shard_map/broadcast_in_dim | solution.py:198
  7.0 11.5 %all-to-all-start = ((bf16[128,32,128]{2,1,0:T(8,128)(2,1)}), bf16[128,32,128]{2,1,0:T(8,128)(2,1)S(1)}, u32[]{:S(2)}, u32[]{:S(2)}) async-start(bf16[128,32,128]{2,1,0:T(8,128)(2,1)} %broadcast_in_dim.9), calls=%async_computation | async-start | bytes 2097152 | tf_op jit(solution)/shard_map/all_to_all | solution.py:197
  18.5 0.0 copy-done.8
  18.5 0.1 copy.11
  18.6 0.1 reshape.23.visits_ref
  18.7 0.0 copy-done.7
  18.8 0.0 copy-done.3
  18.8 0.0 copy-done.5
  18.8 0.0 copy-done.6
  18.8 0.0 copy-start
  18.8 0.0 copy-start.4
  18.8 19.1 %bucket.1 = (f32[768,256]{1,0:T(8,128)S(1)}, f32[128,128]{1,0:T(8,128)S(1)}) custom-call(s32[128,128]{1,0:T(8,128)S(1)} %bitcast.21, s32[128,128]{1,0:T(8,128)S(1)} %bitcast.23, s32[128,128]{1,0:T(8,128)S(1)} %bitcast.24, f32[2,128,128]{2,1,0:T(8,128)S(1)} %bitcast.20), custom_call_target="tpu_custom_call" | custom-call | flops 8589934592 | bytes 2097152 | tf_op jit(solution)/shard_map/bucket/pallas_call | solution.py:205
  37.9 0.0 copy-start.1
  37.9 0.9 %copy-done.1 = f32[768,256]{1,0:T(8,128)} copy-done((f32[768,256]{1,0:T(8,128)}, f32[768,256]{1,0:T(8,128)S(1)}, u32[]{:S(2)}) %copy-start.1) | copy-done | bytes 786456
  38.9 0.0 all-to-all-done
  38.9 0.0 copy-done
  38.9 0.0 copy-done.4
  38.9 0.0 copy-start.2
  38.9 1.1 %copy-done.2 = f32[768,256]{1,0:T(8,128)S(1)} copy-done((f32[768,256]{1,0:T(8,128)S(1)}, f32[768,256]{1,0:T(8,128)}, u32[]{:S(2)}) %copy-start.2) | copy-done | bytes 786456
  40.0 31.7 %evaluate.1 = f32[128,128]{1,0:T(8,128)} custom-call(s32[512]{0:T(512)S(1)} %reshape.23.visits_ref, bf16[4096,128]{1,0:T(8,128)(2,1)S(1)} %bitcast.19, bf16[256,128]{1,0:T(8,128)(2,1)S(1)} %copy-done.4, bf16[128,64,128]{2,1,0:T(8,128)(2,1)S(1)} %copy-done, f32[768,256]{1,0:T(8,128)S(1)} %copy-done.2, s32[128,128]{1,0:T(8,128)S(1)} %bitcast.22, ...), custom_call_target="tpu_custom_call" | custom-call | tf_op jit(solution)/shard_map/evaluate/pallas_call | solution.py:224
  (1 shorter events, 0.0 us)
Async XLA Ops:
  0.0 18.5 %copy-start.8 = (s32[1,128,4]{1,2,0:T(4,128)S(1)}, s32[1,128,4]{1,2,0:T(4,128)}, u32[]{:S(2)}) copy-start(s32[1,128,4]{1,2,0:T(4,128)} %param.13) | copy-start | bytes 6148
  0.0 18.7 %copy-start.7 = (f32[2,16384]{1,0:T(2,128)S(1)}, f32[2,16384]{1,0:T(2,128)}, u32[]{:S(2)}) copy-start(f32[2,16384]{1,0:T(2,128)} %param.17) | copy-start | bytes 393220
  0.0 18.8 %copy-start.3 = (s32[16384]{0:T(1024)S(1)}, s32[16384]{0:T(1024)}, u32[]{:S(2)}) copy-start(s32[16384]{0:T(1024)} %param.14) | copy-start | bytes 196612
  0.0 18.8 %copy-start.5 = (s32[16384]{0:T(1024)S(1)}, s32[16384]{0:T(1024)}, u32[]{:S(2)}) copy-start(s32[16384]{0:T(1024)} %param.15) | copy-start | bytes 196612
  0.0 18.8 %copy-start.6 = (s32[16384]{0:T(1024)S(1)}, s32[16384]{0:T(1024)}, u32[]{:S(2)}) copy-start(s32[16384]{0:T(1024)} %param.16) | copy-start | bytes 196612
  7.0 31.9 %all-to-all-start = ((bf16[128,32,128]{2,1,0:T(8,128)(2,1)}), bf16[128,32,128]{2,1,0:T(8,128)(2,1)S(1)}, u32[]{:S(2)}, u32[]{:S(2)}) async-start(bf16[128,32,128]{2,1,0:T(8,128)(2,1)} %broadcast_in_dim.9), calls=%async_computation | async-start | bytes 2097152 | tf_op jit(solution)/shard_map/all_to_all | solution.py:197
  18.8 20.1 %copy-start = (bf16[128,64,128]{2,1,0:T(8,128)(2,1)S(1)}, bf16[128,64,128]{2,1,0:T(8,128)(2,1)}, u32[]{:S(2)}) copy-start(bf16[128,64,128]{2,1,0:T(8,128)(2,1)} %constant.5.clone.phi_ref) | copy-start | bytes 6291460
  18.8 20.1 %copy-start.4 = (bf16[256,128]{1,0:T(8,128)(2,1)S(1)}, bf16[256,128]{1,0:T(8,128)(2,1)}, u32[]{:S(2)}) copy-start(bf16[256,128]{1,0:T(8,128)(2,1)} %constant.4.clone.w_ref) | copy-start | bytes 196612
  37.9 0.9 %copy-start.1 = (f32[768,256]{1,0:T(8,128)}, f32[768,256]{1,0:T(8,128)S(1)}, u32[]{:S(2)}) copy-start(f32[768,256]{1,0:T(8,128)S(1)} %get-tuple-element.7.g_ref) | copy-start | bytes 2359300
  38.9 1.1 %copy-start.2 = (f32[768,256]{1,0:T(8,128)S(1)}, f32[768,256]{1,0:T(8,128)}, u32[]{:S(2)}) copy-start(f32[768,256]{1,0:T(8,128)} %copy-done.1) | copy-start | bytes 2359300
where the time goes:
time: 72 us; the launch traced here: 71.8 us
  Pallas kernels  50.9 us (71%)
  starting transfers between devices  11.5 us (16%)
  matrix products  4.72 us (7%)
  local copies, waits for them, and re-layouts  4.54 us (6%)
    pallas_call x1, Pallas kernels, shards(): pl.pallas_call(eval_kernel, out_shape=jax.ShapeDtypeStruct((OWNERS, LANES...  31.7 us
    pallas_call x1, Pallas kernels, shards(): pl.pallas_call(bucket_kernel, out_shape=(jax.ShapeDtypeStruct((ITEMS * OW...  19.1 us
    all_to_all x1, starting transfers between devices, shards(): lax.all_to_all(jnp.broadcast_to(coeffs[None], (OWNERS, SHARDS, LANES)), M...  11.5 us
    dot_general x1, matrix products, shards(): jnp.einsum('kcl,klt->tkc', weighted, wigner[0], preferred_element_type=F32)  4.72 us
    unnamed x20, local copies, waits for them, and re-layouts  2.2 us
    broadcast_in_dim x2, local copies, waits for them, and re-layouts, shards(): jnp.broadcast_to(coeffs[None], (OWNERS, SHARDS, LANES))  1.76 us
  transfers between devices with their start and end apart: 1, of which 0 were waited for; matrix products, arithmetic and copies ran while one was open for 0% of the time, Pallas kernels for 27%

commit v1 on v0

v1 whole, which is shorter than its diff:
```python
import math

import jax
import jax.numpy as jnp
import numpy as np
from jax import lax
from jax.experimental import pallas as pl
from jax.experimental.pallas import tpu as pltpu
from jax.sharding import PartitionSpec as P

BF = jnp.bfloat16
F32 = jnp.float32
MESH_AXES = ("order", "shard")
NPHI = 4096
NPSI = 128
MODES = 32
ORDERS = 64
GROUPS = 4
SHARDS = 32
OWNERS = 128
LANES = 128
RANKS = 192
WIDE = 256
ITEMS = 4
LOCAL = 16
DEGREES = 2048
REPEAT = 16
MIB = 1024 * 1024
NT = (((1,), (1,)), ((), ()))


def phi_tables():
    phi = np.arange(NPHI, dtype=np.int64)[:, None]
    mode = np.arange(MODES, dtype=np.int64)[None, :]
    phase = ((phi * mode) % NPHI).astype(np.float64) * (2.0 * math.pi / NPHI)
    both = np.concatenate([np.cos(phase), -np.sin(phase)], axis=1)
    blocks = both.reshape(NPHI // 32, 32, 2 * MODES).transpose(0, 2, 1)
    return np.tile(blocks, (1, 1, 4)).astype(jnp.bfloat16)


def psi_tables():
    psi = np.arange(NPSI, dtype=np.int64)[:, None]
    order = np.arange(ORDERS, dtype=np.int64)[None, :]
    phase = ((psi * order) % NPSI).astype(np.float64) * (2.0 * math.pi / NPSI)
    cos, sin = np.cos(phase), np.sin(phase)
    real = np.stack([cos, -sin], axis=2).reshape(NPSI, 2 * ORDERS)
    imag = np.stack([sin, cos], axis=2).reshape(NPSI, 2 * ORDERS)
    return np.concatenate([real, imag], axis=0).astype(jnp.bfloat16)


def iota_bf(shape, dim):
    return lax.broadcasted_iota(jnp.int32, shape, dim).astype(F32).astype(BF)


def coeff_kernel(
    sky_hbm, beam_hbm, wigner_hbm, out_hbm, sky_ref, beam_ref, wigner, mixed, turned, copies, small, large, outs
):
    half = LOCAL // 2
    first = [
        pltpu.make_async_copy(sky_hbm, sky_ref, small.at[0]),
        pltpu.make_async_copy(beam_hbm, beam_ref, small.at[1]),
    ]
    loads = [
        pltpu.make_async_copy(
            wigner_hbm.at[0, pl.ds(i * half, half)], wigner.at[pl.ds(i * half, half)], large.at[i]
        )
        for i in range(2)
    ]
    for copy in first + loads:
        copy.start()
    for copy in first:
        copy.wait()
    sky = sky_ref[0]
    for i in range(2):
        loads[i].wait()
        for k in range(i * half, (i + 1) * half):
            weighted = (sky * beam_ref[k : k + 1, :]).astype(BF)
            mixed[2 * k : 2 * k + 2, :] = jnp.dot(weighted, wigner[k], preferred_element_type=F32)
    turned[...] = mixed[...].T
    block = jnp.concatenate(
        [turned[pl.ds(row, SHARDS, stride=4), :] for row in range(4)], axis=1
    ).astype(BF)
    for i in range(REPEAT):
        copies[i] = block
    sends = [
        pltpu.make_async_copy(copies, out_hbm.at[pl.ds(i * REPEAT, REPEAT)], outs.at[i])
        for i in range(OWNERS // REPEAT)
    ]
    for copy in sends:
        copy.start()
    for copy in sends:
        copy.wait()


def bucket_kernel(slot_ref, phi_ref, psi_ref, frac_ref, g_ref, rank_ref, carry, lhs, hot):
    zero = jnp.zeros((), BF)
    one = jnp.ones((), BF)
    own_iota = iota_bf((OWNERS, LANES), 0)
    own_wide = lax.broadcasted_iota(jnp.int32, (OWNERS, LANES), 0)
    rank_iota = iota_bf((RANKS, LANES), 0)
    before = (
        lax.broadcasted_iota(jnp.int32, (LANES, 2 * LANES), 0)
        < lax.broadcasted_iota(jnp.int32, (LANES, 2 * LANES), 1)
    ).astype(F32).astype(BF)
    carry[...] = jnp.zeros_like(carry)
    g_ref[...] = jnp.zeros_like(g_ref)

    def block(step, _):
        start = pl.multiple_of(step * 8, 8)
        slots = slot_ref[pl.ds(start, 8), :]
        owners = slots >> 2
        names = owners.astype(F32)
        rows = ((slots & 3) * 32 + phi_ref[pl.ds(start, 8), :]).astype(F32)
        psis = psi_ref[pl.ds(start, 8), :].astype(F32)
        seen = carry[...]
        ranks = []
        for u in range(8):
            mask = own_iota == names[u : u + 1].astype(BF)
            count = jnp.dot(jnp.where(mask, one, zero), before, preferred_element_type=F32)
            place = count[:, :LANES] + seen
            seen = seen + count[:, LANES:]
            rank = jnp.sum(
                jnp.where(own_wide == owners[u : u + 1], place, 0.0), axis=0, keepdims=True
            )
            ranks.append(rank)
            cut = slice(u * LANES, (u + 1) * LANES)
            hot[:, cut] = jnp.where(rank_iota == rank.astype(BF), one, zero)
            along = pl.ds(pl.multiple_of((start + u) * LANES, LANES), LANES)
            items = (rows[u : u + 1], psis[u : u + 1], frac_ref[0:1, along], frac_ref[1:2, along])
            for n, item in enumerate(items):
                lhs[n * OWNERS : (n + 1) * OWNERS, cut] = jnp.where(mask, item.astype(BF), zero)
        carry[...] = seen
        rank_ref[pl.ds(start, 8), :] = jnp.concatenate(ranks, axis=0)
        g_ref[...] += lax.dot_general(lhs[...], hot[...], NT, preferred_element_type=F32)
        return 0

    lax.fori_loop(0, 16, block, 0, unroll=4)


def eval_kernel(
    visits_ref,
    coeff_hbm,
    w_hbm,
    phi_hbm,
    g_hbm,
    slot_hbm,
    rank_hbm,
    out_ref,
    narrow,
    coeff,
    w_ref,
    phi_ref,
    g_ref,
    slot_ref,
    rank_ref,
    spec,
    tile_ref,
    found,
    parts,
    whole,
):
    quarter = OWNERS * SHARDS // 4
    pieces = [
        pltpu.make_async_copy(
            coeff_hbm.at[pl.ds(i * quarter, quarter)], narrow.at[pl.ds(i * quarter, quarter)], parts.at[i]
        )
        for i in range(4)
    ]
    others = [
        pltpu.make_async_copy(source, target, whole.at[i])
        for i, (source, target) in enumerate(
            ((w_hbm, w_ref), (phi_hbm, phi_ref), (g_hbm, g_ref), (slot_hbm, slot_ref), (rank_hbm, rank_ref))
        )
    ]
    for copy in pieces + others:
        copy.start()
    zero = jnp.zeros((), BF)
    one = jnp.ones((), BF)
    lane = lax.broadcasted_iota(jnp.int32, (1, LANES), 1) // 32

    for i in range(4):
        pieces[i].wait()

        def widen(step, _):
            start = pl.multiple_of(i * quarter + step * 256, 256)
            coeff[pl.ds(start, 256), :] = narrow[pl.ds(start, 256), :].astype(F32)
            return 0

        lax.fori_loop(0, 4, widen, 0, unroll=2)

    def spectrum(step, _):
        blocks = []
        for v in range(2):
            block = coeff[pl.ds(step * 2 + v, LANES, stride=SHARDS), :]
            turned = [block] + [pltpu.roll(block, 32 * n, axis=1) for n in (1, 2, 3)]
            for row in range(4):
                part = None
                for o in range(4):
                    piece = turned[(o - row) % 4][o * 32 : (o + 1) * 32]
                    part = piece if part is None else jnp.where(lane == o, piece, part)
                blocks.append(part.astype(BF))
        block = jnp.concatenate(blocks, axis=0)
        both = lax.dot_general(w_ref[...], block, NT, preferred_element_type=F32).astype(BF)
        for v in range(2):
            cut = both[:, v * LANES : (v + 1) * LANES]
            spec[step * 2 + v] = jnp.concatenate([cut[:NPSI], cut[NPSI:]], axis=1)
        return 0

    others[0].wait()
    lax.fori_loop(0, SHARDS // 2, spectrum, 0, unroll=4)

    def tiles(s, _):
        source = spec[s]
        for pair in range(2):
            chosen = []
            for o in (2 * pair, 2 * pair + 1):
                waves, lane_row = None, None
                for j in range(4):
                    tile = jnp.maximum(visits_ref[(o * SHARDS + s) * 4 + j], 0)
                    wave = phi_ref[o * 32 + (tile & 31)]
                    row = jnp.full((1, LANES), tile >> 5, jnp.int32)
                    waves = wave if j == 0 else jnp.where(lane == j, wave, waves)
                    lane_row = row if j == 0 else jnp.where(lane == j, row, lane_row)
                chosen.append(
                    jnp.concatenate(
                        [
                            jnp.where(lane_row == row, waves[c * 32 : (c + 1) * 32], zero)
                            for c in range(2)
                            for row in range(4)
                        ],
                        axis=0,
                    )
                )
            cells = jnp.dot(source, jnp.concatenate(chosen, axis=1), preferred_element_type=F32)
            for v in range(2):
                tile_ref[(2 * pair + v) * SHARDS + s] = cells[:, v * LANES : (v + 1) * LANES].astype(BF)
        return 0

    others[1].wait()
    lax.fori_loop(0, SHARDS, tiles, 0, unroll=4)

    row_iota = iota_bf((LANES, WIDE), 0)
    pad = jnp.zeros((1, WIDE - RANKS), F32)

    def look(step, _):
        for u in range(32):
            d = step * 32 + u
            at = [
                jnp.concatenate([g_ref[pl.ds(n * OWNERS + d, 1), :], pad], axis=1)
                for n in range(ITEMS)
            ]
            row0 = at[0].astype(BF)
            row1 = (at[0] + 1.0).astype(BF)
            q0 = at[1].astype(BF)
            q1 = jnp.where(at[1] == NPSI - 1.0, 0.0, at[1] + 1.0).astype(BF)
            a0, a1 = (1.0 - at[2]).astype(BF), at[2].astype(BF)
            b0, b1 = (1.0 - at[3]).astype(BF), at[3].astype(BF)
            hot = jnp.where(row_iota == row0, a0, jnp.where(row_iota == row1, a1, zero))
            seen = jnp.dot(tile_ref[d], hot, preferred_element_type=F32)
            weight = jnp.where(row_iota == q0, b0, jnp.where(row_iota == q1, b1, zero))
            found[pl.ds(d, 1), :] = jnp.sum(seen * weight.astype(F32), axis=0, keepdims=True)
        return 0

    others[2].wait()
    lax.fori_loop(0, OWNERS // 32, look, 0)

    others[3].wait()
    others[4].wait()
    rank_iota = iota_bf((RANKS, LANES), 0)
    own_iota = iota_bf((OWNERS, LANES), 0)

    def back(step, values):
        start = pl.multiple_of(step * 8, 8)
        owners = (slot_ref[pl.ds(start, 8), :] >> 2).astype(F32)
        ranks = rank_ref[pl.ds(start, 8), :]
        result = []
        for u in range(0, 8, 2):
            hot = jnp.concatenate(
                [
                    jnp.where(rank_iota == ranks[v : v + 1].astype(BF), one, zero)
                    for v in (u, u + 1)
                ],
                axis=1,
            )
            moved = jnp.dot(values, hot, preferred_element_type=F32).astype(BF)
            for v in (u, u + 1):
                part = moved[:, (v - u) * LANES : (v - u + 1) * LANES]
                part = jnp.where(own_iota == owners[v : v + 1].astype(BF), part, zero)
                result.append(jnp.sum(part.astype(F32), axis=0, keepdims=True))
        out_ref[pl.ds(start, 8), :] = jnp.concatenate(result, axis=0)
        return values

    lax.fori_loop(0, 16, back, found[...][:, :RANKS].astype(BF), unroll=4)


def shards(sky_coeffs, beam_coeffs, wigner, visits, point_slot, phi_cell, psi_cell, fraction):
    vmem = pl.BlockSpec(memory_space=pltpu.VMEM)
    anywhere = pl.BlockSpec(memory_space=pl.ANY)
    dma = pltpu.SemaphoreType.DMA
    copies = pl.pallas_call(
        coeff_kernel,
        out_shape=jax.ShapeDtypeStruct((OWNERS, SHARDS, LANES), BF),
        in_specs=[anywhere] * 3,
        out_specs=anywhere,
        scratch_shapes=[
            pltpu.VMEM((1, 2, DEGREES), F32),
            pltpu.VMEM((LOCAL, DEGREES), F32),
            pltpu.VMEM((LOCAL, DEGREES, LANES), BF),
            pltpu.VMEM((2 * LOCAL, LANES), F32),
            pltpu.VMEM((LANES, 2 * LOCAL), F32),
            pltpu.VMEM((REPEAT, SHARDS, LANES), BF),
            dma((2,)),
            dma((2,)),
            dma((OWNERS // REPEAT,)),
        ],
        compiler_params=pltpu.CompilerParams(vmem_limit_bytes=60 * MIB),
        cost_estimate=pl.CostEstimate(
            flops=16 * MIB, bytes_accessed=9 * MIB, transcendentals=0
        ),
        name="coeffs",
    )(sky_coeffs, beam_coeffs, wigner)
    everyone = lax.all_to_all(copies, MESH_AXES, 0, 0, tiled=True)
    slots = point_slot.reshape(OWNERS, LANES)
    grouped, ranks = pl.pallas_call(
        bucket_kernel,
        out_shape=(
            jax.ShapeDtypeStruct((ITEMS * OWNERS, RANKS), F32),
            jax.ShapeDtypeStruct((OWNERS, LANES), F32),
        ),
        in_specs=[vmem] * 4,
        out_specs=(vmem, vmem),
        scratch_shapes=[
            pltpu.VMEM((OWNERS, LANES), F32),
            pltpu.VMEM((ITEMS * OWNERS, 8 * LANES), BF),
            pltpu.VMEM((RANKS, 8 * LANES), BF),
        ],
        compiler_params=pltpu.CompilerParams(vmem_limit_bytes=24 * MIB),
        cost_estimate=pl.CostEstimate(
            flops=8 * 1024 * MIB, bytes_accessed=2 * MIB, transcendentals=0
        ),
        name="bucket",
    )(slots, phi_cell.reshape(OWNERS, LANES), psi_cell.reshape(OWNERS, LANES), fraction)
    timeline = pl.pallas_call(
        eval_kernel,
        out_shape=jax.ShapeDtypeStruct((OWNERS, LANES), F32),
        in_specs=[pl.BlockSpec(memory_space=pltpu.SMEM)] + [anywhere] * 6,
        out_specs=vmem,
        scratch_shapes=[
            pltpu.VMEM((OWNERS * SHARDS, LANES), BF),
            pltpu.VMEM((OWNERS * SHARDS, LANES), F32),
            pltpu.VMEM((2 * NPSI, LANES), BF),
            pltpu.VMEM((NPHI // 32, 2 * MODES, LANES), BF),
            pltpu.VMEM((ITEMS * OWNERS, RANKS), F32),
            pltpu.VMEM((OWNERS, LANES), jnp.int32),
            pltpu.VMEM((OWNERS, LANES), F32),
            pltpu.VMEM((SHARDS, NPSI, 2 * LANES), BF),
            pltpu.VMEM((OWNERS, NPSI, LANES), BF),
            pltpu.VMEM((OWNERS, WIDE), F32),
            dma((4,)),
            dma((5,)),
        ],
        compiler_params=pltpu.CompilerParams(vmem_limit_bytes=60 * MIB),
        cost_estimate=pl.CostEstimate(
            flops=8 * 1024 * MIB, bytes_accessed=4 * MIB, transcendentals=0
        ),
        name="evaluate",
    )(
        visits.reshape(-1),
        everyone.reshape(OWNERS * SHARDS, LANES),
        jnp.asarray(psi_tables()),
        jnp.asarray(phi_tables()),
        grouped,
        slots,
        ranks,
    )
    return timeline.reshape(-1)


def solution(mesh):
    placed = (
        P("shard", None, None),
        P("order", None),
        P("shard", "order", None, None),
        P(("order", "shard"), None, None),
        P(("order", "shard")),
        P(("order", "shard")),
        P(("order", "shard")),
        P(None, ("order", "shard")),
    )
    return jax.shard_map(
        shards, mesh=mesh, in_specs=placed, out_specs=P(("order", "shard")), check_vma=False
    )
```

time: 72 us -> 55 us (0.76)
  Pallas kernels: 50.9 us -> 33.3 us
  waiting for transfers between devices: 0.01 us -> 6.71 us
  matrix products: 4.72 us -> 0 us
  local copies, waits for them, and re-layouts: 4.54 us -> 3.26 us
    pallas_call x1, Pallas kernels: 31.7 us -> 17.9 us  [shards(): pl.pallas_call(eval_kernel, out_shape=jax.ShapeDtypeStruct((OWNERS, LANES...]
    pallas_call x1, Pallas kernels: 19.1 us -> 9.89 us  [shards(): pl.pallas_call(bucket_kernel, out_shape=(jax.ShapeDtypeStruct((ITEMS * OW...]
    all_to_all x1, waiting for transfers between devices: 0.01 us -> 6.71 us  [shards(): everyone = lax.all_to_all(copies, MESH_AXES, 0, 0, tiled=True)]
    pallas_call x0 -> x1, Pallas kernels: none -> 5.5 us  [shards(): pl.pallas_call(coeff_kernel, out_shape=jax.ShapeDtypeStruct((OWNERS, SHAR...]
    dot_general x1 -> x0, matrix products: 4.72 us -> none  [shards(): jnp.einsum('kcl,klt->tkc', weighted, wigner[0], preferred_element_type=F32)]
    broadcast_in_dim x2 -> x0, local copies, waits for them, and re-layouts: 1.76 us -> none  [shards(): jnp.broadcast_to(coeffs[None], (OWNERS, SHARDS, LANES))]
    unnamed x20 -> x17, local copies, waits for them, and re-layouts: 2.2 us -> 2.56 us
  transfers between devices with their start and end apart: 1 -> 1, of which waited for: 0 -> 1; matrix products, arithmetic and copies ran while one was open for 0% -> 1% of each run, Pallas kernels for 27% -> 18%
where the time goes in v1:
time: 55 us; the launch traced here: 54.8 us
  Pallas kernels  33.3 us (61%)
  starting transfers between devices  11.5 us (21%)
  waiting for transfers between devices  6.71 us (12%)
  local copies, waits for them, and re-layouts  3.26 us (6%)
    pallas_call x1, Pallas kernels, shards(): pl.pallas_call(eval_kernel, out_shape=jax.ShapeDtypeStruct((OWNERS, LANES...  17.9 us
    all_to_all x1, starting transfers between devices, shards(): everyone = lax.all_to_all(copies, MESH_AXES, 0, 0, tiled=True)  11.5 us
    pallas_call x1, Pallas kernels, shards(): pl.pallas_call(bucket_kernel, out_shape=(jax.ShapeDtypeStruct((ITEMS * OW...  9.89 us
    all_to_all x1, waiting for transfers between devices, shards(): everyone = lax.all_to_all(copies, MESH_AXES, 0, 0, tiled=True)  6.71 us
    pallas_call x1, Pallas kernels, shards(): pl.pallas_call(coeff_kernel, out_shape=jax.ShapeDtypeStruct((OWNERS, SHAR...  5.5 us
    unnamed x17, local copies, waits for them, and re-layouts  2.56 us
  transfers between devices with their start and end apart: 1, of which 1 were waited for; matrix products, arithmetic and copies ran while one was open for 1% of the time, Pallas kernels for 18%

profile of v1, /device:TPU:1, one launch (start us, length us, event | category | flops | bytes accessed | tf_op | source)
XLA Modules:
  0.0 54.8 jit_solution(16457597209491074723)
XLA Ops:
  0.0 0.0 copy-start.7
  0.0 0.0 copy-start.3
  0.0 0.0 copy-start.1
  0.0 0.0 copy-start.2
  0.0 0.0 copy-start
  0.0 5.5 %coeffs.1 = bf16[128,32,128]{2,1,0:T(8,128)(2,1)} custom-call(f32[1,2,2048]{2,1,0:T(2,128)} %sky_hbm.1, f32[16,2048]{1,0:T(8,128)} %beam_hbm.1, bf16[1,16,2048,128]{3,2,1,0:T(8,128)(2,1)} %wigner_hbm.1), custom_call_target="tpu_custom_call" | custom-call | flops 16777216 | bytes 9437184 | tf_op jit(solution)/shard_map/coeffs/pallas_call | solution.py:300
  5.5 11.5 %all-to-all-start = ((bf16[128,32,128]{2,1,0:T(8,128)(2,1)}), bf16[128,32,128]{2,1,0:T(8,128)(2,1)S(1)}, u32[]{:S(2)}, u32[]{:S(2)}) async-start(bf16[128,32,128]{2,1,0:T(8,128)(2,1)} %coeffs.1), calls=%async_computation | async-start | bytes 2097152 | tf_op jit(solution)/shard_map/all_to_all | solution.py:322
  17.1 0.0 copy-done.7
  17.1 0.1 copy.11
  17.2 0.7 %reshape.18.visits_ref = s32[512]{0:T(512)} reshape(s32[1,128,4]{2,1,0:T(8,128)S(1)} %copy.11) | data formatting | bytes 4096 | tf_op jit(solution)/shard_map/reshape | solution.py:368
  17.9 0.0 copy-done.3
  17.9 0.0 copy-done.1
  17.9 0.0 copy-done.2
  17.9 0.0 copy-done
  17.9 9.9 %bucket.1 = (f32[512,192]{1,0:T(8,128)S(1)}, f32[128,128]{1,0:T(8,128)S(1)}) custom-call(s32[128,128]{1,0:T(8,128)S(1)} %bitcast.8, s32[128,128]{1,0:T(8,128)S(1)} %bitcast.5, s32[128,128]{1,0:T(8,128)S(1)} %bitcast.6, f32[2,16384]{1,0:T(2,128)S(1)} %copy-done), custom_call_target="tpu_custom_call" | custom-call | flops 8589934592 | bytes 2097152 | tf_op jit(solution)/shard_map/bucket/pallas_call | solution.py:324
  27.8 0.0 copy-start.4
  27.8 0.8 %copy-done.4 = f32[512,192]{1,0:T(8,128)} copy-done((f32[512,192]{1,0:T(8,128)}, f32[512,192]{1,0:T(8,128)S(1)}, u32[]{:S(2)}) %copy-start.4) | copy-done | bytes 393240
  28.6 0.0 copy-start.5
  28.6 0.6 %copy-done.5 = f32[128,128]{1,0:T(8,128)} copy-done((f32[128,128]{1,0:T(8,128)}, f32[128,128]{1,0:T(8,128)S(1)}, u32[]{:S(2)}) %copy-start.5) | copy-done | bytes 65560
  29.2 6.7 %all-to-all-done = bf16[128,32,128]{2,1,0:T(8,128)(2,1)S(1)} async-done(((bf16[128,32,128]{2,1,0:T(8,128)(2,1)}), bf16[128,32,128]{2,1,0:T(8,128)(2,1)S(1)}, u32[]{:S(2)}, u32[]{:S(2)}) %all-to-all-start) | async-done | bytes 1048608 | tf_op jit(solution)/shard_map/all_to_all | solution.py:322
  36.0 0.0 copy-start.6
  36.0 1.0 %copy-done.6 = bf16[128,32,128]{2,1,0:T(8,128)(2,1)} copy-done((bf16[128,32,128]{2,1,0:T(8,128)(2,1)}, bf16[128,32,128]{2,1,0:T(8,128)(2,1)S(1)}, u32[]{:S(2)}) %copy-start.6) | copy-done | bytes 1048600
  36.9 17.9 %evaluate.1 = f32[128,128]{1,0:T(8,128)} custom-call(s32[512]{0:T(512)} %reshape.18.visits_ref, bf16[4096,128]{1,0:T(8,128)(2,1)} %bitcast.9, bf16[256,128]{1,0:T(8,128)(2,1)} %constant.4.clone.w_hbm, bf16[128,64,128]{2,1,0:T(8,128)(2,1)} %constant.5.clone.phi_hbm, f32[512,192]{1,0:T(8,128)} %copy-done.4, s32[128,128]{1,0:T(8,128)} %bitcast.7, ...), custom_call_target="tpu_custom_call" | custom-call | flops 8589934592 | bytes 4194304 | tf_op jit(solution)/shard_map/evaluate/pallas_call | solution.py:343
Async XLA Ops:
  0.0 17.1 %copy-start.7 = (s32[1,128,4]{1,2,0:T(4,128)S(1)}, s32[1,128,4]{1,2,0:T(4,128)}, u32[]{:S(2)}) copy-start(s32[1,128,4]{1,2,0:T(4,128)} %param.13) | copy-start | bytes 6148
  0.0 17.9 %copy-start.3 = (s32[16384]{0:T(1024)S(1)}, s32[16384]{0:T(1024)}, u32[]{:S(2)}) copy-start(s32[16384]{0:T(1024)} %param.14) | copy-start | bytes 196612
  0.0 17.9 %copy-start.1 = (s32[16384]{0:T(1024)S(1)}, s32[16384]{0:T(1024)}, u32[]{:S(2)}) copy-start(s32[16384]{0:T(1024)} %param.15) | copy-start | bytes 196612
  0.0 17.9 %copy-start.2 = (s32[16384]{0:T(1024)S(1)}, s32[16384]{0:T(1024)}, u32[]{:S(2)}) copy-start(s32[16384]{0:T(1024)} %param.16) | copy-start | bytes 196612
  0.0 17.9 %copy-start = (f32[2,16384]{1,0:T(2,128)S(1)}, f32[2,16384]{1,0:T(2,128)}, u32[]{:S(2)}) copy-start(f32[2,16384]{1,0:T(2,128)} %frac_ref.1) | copy-start | bytes 393220
  5.5 30.4 %all-to-all-start = ((bf16[128,32,128]{2,1,0:T(8,128)(2,1)}), bf16[128,32,128]{2,1,0:T(8,128)(2,1)S(1)}, u32[]{:S(2)}, u32[]{:S(2)}) async-start(bf16[128,32,128]{2,1,0:T(8,128)(2,1)} %coeffs.1), calls=%async_computation | async-start | bytes 2097152 | tf_op jit(solution)/shard_map/all_to_all | solution.py:322
  27.8 0.8 %copy-start.4 = (f32[512,192]{1,0:T(8,128)}, f32[512,192]{1,0:T(8,128)S(1)}, u32[]{:S(2)}) copy-start(f32[512,192]{1,0:T(8,128)S(1)} %get-tuple-element.7.g_hbm) | copy-start | bytes 1179652
  28.6 0.6 %copy-start.5 = (f32[128,128]{1,0:T(8,128)}, f32[128,128]{1,0:T(8,128)S(1)}, u32[]{:S(2)}) copy-start(f32[128,128]{1,0:T(8,128)S(1)} %get-tuple-element.8.rank_hbm) | copy-start | bytes 196612
  36.0 1.0 %copy-start.6 = (bf16[128,32,128]{2,1,0:T(8,128)(2,1)}, bf16[128,32,128]{2,1,0:T(8,128)(2,1)S(1)}, u32[]{:S(2)}) copy-start(bf16[128,32,128]{2,1,0:T(8,128)(2,1)S(1)} %all-to-all-done) | copy-start | bytes 3145732

commit v2 on v1

--- a/solution.py
+++ b/solution.py
@@ -25,7 +25,10 @@
 LOCAL = 16
 DEGREES = 2048
 REPEAT = 16
+CHIPS = 64
+PEERS = [[core + 2 * chip for chip in range(CHIPS)] for core in range(2)]
 MIB = 1024 * 1024
+UNROLL = 2
 NT = (((1,), (1,)), ((), ()))
 
 
@@ -34,6 +37,7 @@
     mode = np.arange(MODES, dtype=np.int64)[None, :]
     phase = ((phi * mode) % NPHI).astype(np.float64) * (2.0 * math.pi / NPHI)
     both = np.concatenate([np.cos(phase), -np.sin(phase)], axis=1)
+    both = both.reshape(NPHI, 2, MODES // 2, 2).transpose(0, 1, 3, 2)
     blocks = both.reshape(NPHI // 32, 32, 2 * MODES).transpose(0, 2, 1)
     return np.tile(blocks, (1, 1, 4)).astype(jnp.bfloat16)
 
@@ -84,7 +88,7 @@
         copies[i] = block
     sends = [
         pltpu.make_async_copy(copies, out_hbm.at[pl.ds(i * REPEAT, REPEAT)], outs.at[i])
-        for i in range(OWNERS // REPEAT)
+        for i in range(CHIPS // REPEAT)
     ]
     for copy in sends:
         copy.start()
@@ -131,7 +135,7 @@
                 lhs[n * OWNERS : (n + 1) * OWNERS, cut] = jnp.where(mask, item.astype(BF), zero)
         carry[...] = seen
         rank_ref[pl.ds(start, 8), :] = jnp.concatenate(ranks, axis=0)
-        g_ref[...] += lax.dot_general(lhs[...], hot[...], NT, preferred_element_type=F32)
+        g_ref[:, :RANKS] += lax.dot_general(lhs[...], hot[...], NT, preferred_element_type=F32)
         return 0
 
     lax.fori_loop(0, 16, block, 0, unroll=4)
@@ -139,59 +143,44 @@
 
 def eval_kernel(
     visits_ref,
-    coeff_hbm,
-    w_hbm,
-    phi_hbm,
-    g_hbm,
-    slot_hbm,
-    rank_hbm,
-    out_ref,
-    narrow,
-    coeff,
+    core_ref,
+    mine_ref,
+    theirs_ref,
     w_ref,
     phi_ref,
-    g_ref,
+    g_hbm,
     slot_ref,
     rank_ref,
+    out_ref,
+    coeff,
     spec,
     tile_ref,
     found,
-    parts,
-    whole,
+    g_ref,
+    sem,
 ):
-    quarter = OWNERS * SHARDS // 4
-    pieces = [
-        pltpu.make_async_copy(
-            coeff_hbm.at[pl.ds(i * quarter, quarter)], narrow.at[pl.ds(i * quarter, quarter)], parts.at[i]
-        )
-        for i in range(4)
-    ]
-    others = [
-        pltpu.make_async_copy(source, target, whole.at[i])
-        for i, (source, target) in enumerate(
-            ((w_hbm, w_ref), (phi_hbm, phi_ref), (g_hbm, g_ref), (slot_hbm, slot_ref), (rank_hbm, rank_ref))
-        )
-    ]
-    for copy in pieces + others:
-        copy.start()
+    fetch = pltpu.make_async_copy(g_hbm, g_ref, sem)
+    fetch.start()
     zero = jnp.zeros((), BF)
     one = jnp.ones((), BF)
     lane = lax.broadcasted_iota(jnp.int32, (1, LANES), 1) // 32
 
-    for i in range(4):
-        pieces[i].wait()
+    for i, narrow in enumerate((mine_ref, theirs_ref)):
+        side = core_ref[0] ^ i
 
         def widen(step, _):
-            start = pl.multiple_of(i * quarter + step * 256, 256)
-            coeff[pl.ds(start, 256), :] = narrow[pl.ds(start, 256), :].astype(F32)
+            source = pl.multiple_of(step * 256, 256)
+            place = (step // 2) * 4 + side * 2 + step % 2
+            target = pl.multiple_of(place * 256, 256)
+            coeff[pl.ds(target, 256), :] = narrow[pl.ds(source, 256), :].astype(F32)
             return 0
 
-        lax.fori_loop(0, 4, widen, 0, unroll=2)
-
-    def spectrum(step, _):
+        lax.fori_loop(0, 8, widen, 0, unroll=2)
+
+    def spectrum(pair):
         blocks = []
         for v in range(2):
-            block = coeff[pl.ds(step * 2 + v, LANES, stride=SHARDS), :]
+            block = coeff[pl.ds(pair * 2 + v, LANES, stride=SHARDS), :]
             turned = [block] + [pltpu.roll(block, 32 * n, axis=1) for n in (1, 2, 3)]
             for row in range(4):
                 part = None
@@ -203,20 +192,16 @@
         both = lax.dot_general(w_ref[...], block, NT, preferred_element_type=F32).astype(BF)
         for v in range(2):
             cut = both[:, v * LANES : (v + 1) * LANES]
-            spec[step * 2 + v] = jnp.concatenate([cut[:NPSI], cut[NPSI:]], axis=1)
-        return 0
-
-    others[0].wait()
-    lax.fori_loop(0, SHARDS // 2, spectrum, 0, unroll=4)
-
-    def tiles(s, _):
+            spec[pair * 2 + v] = jnp.concatenate([cut[:NPSI], cut[NPSI:]], axis=1)
+
+    def tiles(s):
         source = spec[s]
         for pair in range(2):
             chosen = []
             for o in (2 * pair, 2 * pair + 1):
                 waves, lane_row = None, None
                 for j in range(4):
-                    tile = jnp.maximum(visits_ref[(o * SHARDS + s) * 4 + j], 0)
+                    tile = jnp.maximum(visits_ref[j, o * SHARDS + s], 0)
                     wave = phi_ref[o * 32 + (tile & 31)]
                     row = jnp.full((1, LANES), tile >> 5, jnp.int32)
                     waves = wave if j == 0 else jnp.where(lane == j, wave, waves)
@@ -233,22 +218,14 @@
                 )
             cells = jnp.dot(source, jnp.concatenate(chosen, axis=1), preferred_element_type=F32)
             for v in range(2):
-                tile_ref[(2 * pair + v) * SHARDS + s] = cells[:, v * LANES : (v + 1) * LANES].astype(BF)
-        return 0
-
-    others[1].wait()
-    lax.fori_loop(0, SHARDS, tiles, 0, unroll=4)
+                tile_ref[s * 4 + 2 * pair + v] = cells[:, v * LANES : (v + 1) * LANES].astype(BF)
 
     row_iota = iota_bf((LANES, WIDE), 0)
-    pad = jnp.zeros((1, WIDE - RANKS), F32)
-
-    def look(step, _):
-        for u in range(32):
-            d = step * 32 + u
-            at = [
-                jnp.concatenate([g_ref[pl.ds(n * OWNERS + d, 1), :], pad], axis=1)
-                for n in range(ITEMS)
-            ]
+
+    def look(s):
+        for o in range(4):
+            d = o * SHARDS + s
+            at = [g_ref[pl.ds(n * OWNERS + d, 1), :] for n in range(ITEMS)]
             row0 = at[0].astype(BF)
             row1 = (at[0] + 1.0).astype(BF)
             q0 = at[1].astype(BF)
@@ -256,16 +233,31 @@
             a0, a1 = (1.0 - at[2]).astype(BF), at[2].astype(BF)
             b0, b1 = (1.0 - at[3]).astype(BF), at[3].astype(BF)
             hot = jnp.where(row_iota == row0, a0, jnp.where(row_iota == row1, a1, zero))
-            seen = jnp.dot(tile_ref[d], hot, preferred_element_type=F32)
+            seen = jnp.dot(tile_ref[s * 4 + o], hot, preferred_element_type=F32)
             weight = jnp.where(row_iota == q0, b0, jnp.where(row_iota == q1, b1, zero))
             found[pl.ds(d, 1), :] = jnp.sum(seen * weight.astype(F32), axis=0, keepdims=True)
+
+    def work(pair, stages):
+        if 2 in stages:
+            for v in range(2):
+                look((pair - 2) * 2 + v)
+        if 1 in stages:
+            for v in range(2):
+                tiles((pair - 1) * 2 + v)
+        if 0 in stages:
+            spectrum(pair)
+
+    def turn(pair, _):
+        work(pair, (0, 1, 2))
         return 0
 
-    others[2].wait()
-    lax.fori_loop(0, OWNERS // 32, look, 0)
-
-    others[3].wait()
-    others[4].wait()
+    work(0, (0,))
+    work(1, (0, 1))
+    fetch.wait()
+    lax.fori_loop(2, SHARDS // 2, turn, 0, unroll=UNROLL)
+    work(SHARDS // 2, (1, 2))
+    work(SHARDS // 2 + 1, (2,))
+
     rank_iota = iota_bf((RANKS, LANES), 0)
     own_iota = iota_bf((OWNERS, LANES), 0)
 
@@ -299,7 +291,7 @@
     dma = pltpu.SemaphoreType.DMA
     copies = pl.pallas_call(
         coeff_kernel,
-        out_shape=jax.ShapeDtypeStruct((OWNERS, SHARDS, LANES), BF),
+        out_shape=jax.ShapeDtypeStruct((CHIPS, SHARDS, LANES), BF),
         in_specs=[anywhere] * 3,
         out_specs=anywhere,
         scratch_shapes=[
@@ -311,7 +303,7 @@
             pltpu.VMEM((REPEAT, SHARDS, LANES), BF),
             dma((2,)),
             dma((2,)),
-            dma((OWNERS // REPEAT,)),
+            dma((CHIPS // REPEAT,)),
         ],
         compiler_params=pltpu.CompilerParams(vmem_limit_bytes=60 * MIB),
         cost_estimate=pl.CostEstimate(
@@ -319,12 +311,13 @@
         ),
         name="coeffs",
     )(sky_coeffs, beam_coeffs, wigner)
-    everyone = lax.all_to_all(copies, MESH_AXES, 0, 0, tiled=True)
+    mine = lax.all_to_all(copies, MESH_AXES, 0, 0, axis_index_groups=PEERS, tiled=True)
+    core = jnp.full((1,), lax.axis_index("shard") & 1, jnp.int32)
     slots = point_slot.reshape(OWNERS, LANES)
     grouped, ranks = pl.pallas_call(
         bucket_kernel,
         out_shape=(
-            jax.ShapeDtypeStruct((ITEMS * OWNERS, RANKS), F32),
+            jax.ShapeDtypeStruct((ITEMS * OWNERS, WIDE), F32),
             jax.ShapeDtypeStruct((OWNERS, LANES), F32),
         ),
         in_specs=[vmem] * 4,
@@ -334,39 +327,37 @@
             pltpu.VMEM((ITEMS * OWNERS, 8 * LANES), BF),
             pltpu.VMEM((RANKS, 8 * LANES), BF),
         ],
-        compiler_params=pltpu.CompilerParams(vmem_limit_bytes=24 * MIB),
+        compiler_params=pltpu.CompilerParams(vmem_limit_bytes=12 * MIB),
         cost_estimate=pl.CostEstimate(
             flops=8 * 1024 * MIB, bytes_accessed=2 * MIB, transcendentals=0
         ),
         name="bucket",
     )(slots, phi_cell.reshape(OWNERS, LANES), psi_cell.reshape(OWNERS, LANES), fraction)
+    mine, ranks = lax.optimization_barrier((mine, ranks))
+    theirs = lax.ppermute(mine, "shard", [(n, n ^ 1) for n in range(SHARDS)])
     timeline = pl.pallas_call(
         eval_kernel,
         out_shape=jax.ShapeDtypeStruct((OWNERS, LANES), F32),
-        in_specs=[pl.BlockSpec(memory_space=pltpu.SMEM)] + [anywhere] * 6,
+        in_specs=[pl.BlockSpec(memory_space=pltpu.SMEM)] * 2 + [vmem] * 4 + [anywhere] + [vmem] * 2,
         out_specs=vmem,
         scratch_shapes=[
-            pltpu.VMEM((OWNERS * SHARDS, LANES), BF),
             pltpu.VMEM((OWNERS * SHARDS, LANES), F32),
-            pltpu.VMEM((2 * NPSI, LANES), BF),
-            pltpu.VMEM((NPHI // 32, 2 * MODES, LANES), BF),
-            pltpu.VMEM((ITEMS * OWNERS, RANKS), F32),
-            pltpu.VMEM((OWNERS, LANES), jnp.int32),
-            pltpu.VMEM((OWNERS, LANES), F32),
             pltpu.VMEM((SHARDS, NPSI, 2 * LANES), BF),
             pltpu.VMEM((OWNERS, NPSI, LANES), BF),
             pltpu.VMEM((OWNERS, WIDE), F32),
-            dma((4,)),
-            dma((5,)),
+            pltpu.VMEM((ITEMS * OWNERS, WIDE), F32),
+            dma,
         ],
-        compiler_params=pltpu.CompilerParams(vmem_limit_bytes=60 * MIB),
+        compiler_params=pltpu.CompilerParams(vmem_limit_bytes=24 * MIB),
         cost_estimate=pl.CostEstimate(
             flops=8 * 1024 * MIB, bytes_accessed=4 * MIB, transcendentals=0
         ),
         name="evaluate",
     )(
-        visits.reshape(-1),
-        everyone.reshape(OWNERS * SHARDS, LANES),
+        visits[0].T,
+        core,
+        mine.reshape(CHIPS * SHARDS, LANES),
+        theirs.reshape(CHIPS * SHARDS, LANES),
         jnp.asarray(psi_tables()),
         jnp.asarray(phi_tables()),
         grouped,

time: 55 us -> 48.1 us (0.87)
  Pallas kernels: 33.3 us -> 29.1 us
  waiting for transfers between devices: 6.71 us -> 2.6 us
  starting transfers between devices: 11.5 us -> 14.3 us
  local copies, waits for them, and re-layouts: 3.26 us -> 1.87 us
    all_to_all x1, waiting for transfers between devices: 6.71 us -> 1.07 us  [shards(): lax.all_to_all(copies, MESH_AXES, 0, 0, axis_index_groups=PEERS, tiled=True)]
    pallas_call x1, Pallas kernels: 17.9 us -> 13.8 us  [shards(): pl.pallas_call(eval_kernel, out_shape=jax.ShapeDtypeStruct((OWNERS, LANES...]
    ppermute x0 -> x1, starting transfers between devices: none -> 2.29 us  [shards(): theirs = lax.ppermute(mine, 'shard', [(n, n ^ 1) for n in range(SHARDS)])]
    ppermute x0 -> x1, waiting for transfers between devices: none -> 1.54 us  [shards(): theirs = lax.ppermute(mine, 'shard', [(n, n ^ 1) for n in range(SHARDS)])]
    reshape x1 -> x0, local copies, waits for them, and re-layouts: 0.7 us -> none  [shards(): visits.reshape(-1)]
    unnamed x17 -> x18, local copies, waits for them, and re-layouts: 2.56 us -> 1.87 us
  transfers between devices with their start and end apart: 1 -> 2, of which waited for: 1 -> 2; matrix products, arithmetic and copies ran while one was open for 1% -> 0% of each run, Pallas kernels for 18% -> 21%
where the time goes in v2:
time: 48.1 us; the launch traced here: 47.9 us
  Pallas kernels  29.1 us (60%)
  starting transfers between devices  14.3 us (30%)
  waiting for transfers between devices  2.6 us (5%)
  local copies, waits for them, and re-layouts  1.87 us (4%)
    pallas_call x1, Pallas kernels, shards(): pl.pallas_call(eval_kernel, out_shape=jax.ShapeDtypeStruct((OWNERS, LANES...  13.8 us
    all_to_all x1, starting transfers between devices, shards(): lax.all_to_all(copies, MESH_AXES, 0, 0, axis_index_groups=PEERS, tiled=True)  12 us
    pallas_call x1, Pallas kernels, shards(): pl.pallas_call(bucket_kernel, out_shape=(jax.ShapeDtypeStruct((ITEMS * OW...  9.98 us
    pallas_call x1, Pallas kernels, shards(): pl.pallas_call(coeff_kernel, out_shape=jax.ShapeDtypeStruct((CHIPS, SHARD...  5.29 us
    ppermute x1, starting transfers between devices, shards(): theirs = lax.ppermute(mine, 'shard', [(n, n ^ 1) for n in range(SHARDS)])  2.29 us
    unnamed x18, local copies, waits for them, and re-layouts  1.87 us
    ppermute x1, waiting for transfers between devices, shards(): theirs = lax.ppermute(mine, 'shard', [(n, n ^ 1) for n in range(SHARDS)])  1.54 us
    all_to_all x1, waiting for transfers between devices, shards(): lax.all_to_all(copies, MESH_AXES, 0, 0, axis_index_groups=PEERS, tiled=True)  1.07 us
  transfers between devices with their start and end apart: 2, of which 2 were waited for; matrix products, arithmetic and copies ran while one was open for 0% of the time, Pallas kernels for 21%

profile of v2, /device:TPU:1, one launch (start us, length us, event | category | flops | bytes accessed | tf_op | source)
XLA Modules:
  0.0 47.9 jit_solution(15073302986655269317)
XLA Ops:
  0.0 0.0 copy-start
  0.0 0.0 copy-start.2
  0.0 0.0 copy-start.1
  0.0 0.0 copy-start.3
  0.0 5.3 %coeffs.1 = bf16[64,32,128]{2,1,0:T(8,128)(2,1)} custom-call(f32[1,2,2048]{2,1,0:T(2,128)} %sky_hbm.1, f32[16,2048]{1,0:T(8,128)} %beam_hbm.1, bf16[1,16,2048,128]{3,2,1,0:T(8,128)(2,1)} %wigner_hbm.1), custom_call_target="tpu_custom_call" | custom-call | flops 16777216 | bytes 9437184 | tf_op jit(solution)/shard_map/coeffs/pallas_call | solution.py:292
  5.3 12.0 %all-to-all-start = ((bf16[64,32,128]{2,1,0:T(8,128)(2,1)}), bf16[64,32,128]{2,1,0:T(8,128)(2,1)S(1)}, u32[]{:S(2)}, u32[]{:S(2)}) async-start(bf16[64,32,128]{2,1,0:T(8,128)(2,1)} %coeffs.1), calls=%async_computation | async-start | bytes 1048576 | tf_op jit(solution)/shard_map/all_to_all | solution.py:314
  17.3 0.0 copy-done
  17.3 0.0 copy-done.2
  17.3 0.0 copy-done.1
  17.3 0.0 copy-done.3
  17.3 0.0 copy-start.4
  17.3 0.0 copy-start.5
  17.4 0.0 copy-start.6
  17.4 10.0 %bucket.1 = (f32[512,256]{1,0:T(8,128)S(1)}, f32[128,128]{1,0:T(8,128)S(1)}) custom-call(s32[128,128]{1,0:T(8,128)S(1)} %bitcast.14, s32[128,128]{1,0:T(8,128)S(1)} %bitcast.12, s32[128,128]{1,0:T(8,128)S(1)} %bitcast.13, f32[2,16384]{1,0:T(2,128)S(1)} %copy-done), custom_call_target="tpu_custom_call" | custom-call | flops 8589934592 | bytes 2097152 | tf_op jit(solution)/shard_map/bucket/pallas_call | solution.py:317
  27.4 0.0 copy-start.7
  27.4 0.8 %copy-done.7 = f32[512,256]{1,0:T(8,128)} copy-done((f32[512,256]{1,0:T(8,128)}, f32[512,256]{1,0:T(8,128)S(1)}, u32[]{:S(2)}) %copy-start.7) | copy-done | bytes 524312
  28.2 1.1 %all-to-all-done = bf16[64,32,128]{2,1,0:T(8,128)(2,1)S(1)} async-done(((bf16[64,32,128]{2,1,0:T(8,128)(2,1)}), bf16[64,32,128]{2,1,0:T(8,128)(2,1)S(1)}, u32[]{:S(2)}, u32[]{:S(2)}) %all-to-all-start) | async-done | bytes 524320 | tf_op jit(solution)/shard_map/all_to_all | solution.py:314
  29.2 2.3 %collective-permute-start = (bf16[64,32,128]{2,1,0:T(8,128)(2,1)S(1)}, bf16[64,32,128]{2,1,0:T(8,128)(2,1)S(1)}, u32[]{:S(2)}, u32[]{:S(2)}) collective-permute-start(bf16[64,32,128]{2,1,0:T(8,128)(2,1)S(1)} %all-to-all-done), channel_id=1, source_target_pairs={{0,1},{1,0},{2,3},{3,2},{4,5},{5,4},{6,7},{7,6},{8,9},{9,8},{10,11... | collective-permute-start | bytes 1572872 | tf_op jit(solution)/shard_map/ppermute | solution.py:337
  31.5 1.5 %collective-permute-done = bf16[64,32,128]{2,1,0:T(8,128)(2,1)S(1)} collective-permute-done((bf16[64,32,128]{2,1,0:T(8,128)(2,1)S(1)}, bf16[64,32,128]{2,1,0:T(8,128)(2,1)S(1)}, u32[]{:S(2)}, u32[]{:S(2)}) %collective-permute-start) | collective-permute-done | bytes 524320 | tf_op jit(solution)/shard_map/ppermute | solution.py:337
  33.1 0.0 copy-done.4
  33.1 0.0 copy-done.5
  33.1 0.0 copy-done.6
  33.1 0.0 copy-start.8
  33.1 1.0 %copy-done.8 = f32[512,256]{1,0:T(8,128)S(1)} copy-done((f32[512,256]{1,0:T(8,128)S(1)}, f32[512,256]{1,0:T(8,128)}, u32[]{:S(2)}) %copy-start.8) | copy-done | bytes 524312
  34.1 13.8 %evaluate.1 = f32[128,128]{1,0:T(8,128)} custom-call(s32[4,128]{1,0:T(4,128)S(1)} %bitcast.16, s32[1]{0:T(128)} %bitcast.2.core_ref, bf16[2048,128]{1,0:T(8,128)(2,1)S(1)} %bitcast.10, bf16[2048,128]{1,0:T(8,128)(2,1)S(1)} %bitcast.11, bf16[256,128]{1,0:T(8,128)(2,1)S(1)} %copy-done.6, bf16[128,64,128]{2,1,0:T(8,128)(2,1)S(1)} %copy-done.5, ...), custom_call_target="tpu_custom_call" | custom-call | flops 8589934592 | bytes 4194304 | tf_op jit(solution)/shard_map/evaluate/pallas_call | solution.py:338
Async XLA Ops:
  0.0 17.3 %copy-start = (f32[2,16384]{1,0:T(2,128)S(1)}, f32[2,16384]{1,0:T(2,128)}, u32[]{:S(2)}) copy-start(f32[2,16384]{1,0:T(2,128)} %frac_ref.1) | copy-start | bytes 393220
  0.0 17.3 %copy-start.2 = (s32[16384]{0:T(1024)S(1)}, s32[16384]{0:T(1024)}, u32[]{:S(2)}) copy-start(s32[16384]{0:T(1024)} %param.16) | copy-start | bytes 196612
  0.0 17.3 %copy-start.1 = (s32[16384]{0:T(1024)S(1)}, s32[16384]{0:T(1024)}, u32[]{:S(2)}) copy-start(s32[16384]{0:T(1024)} %param.15) | copy-start | bytes 196612
  0.0 17.3 %copy-start.3 = (s32[16384]{0:T(1024)S(1)}, s32[16384]{0:T(1024)}, u32[]{:S(2)}) copy-start(s32[16384]{0:T(1024)} %param.14) | copy-start | bytes 196612
  5.3 23.9 %all-to-all-start = ((bf16[64,32,128]{2,1,0:T(8,128)(2,1)}), bf16[64,32,128]{2,1,0:T(8,128)(2,1)S(1)}, u32[]{:S(2)}, u32[]{:S(2)}) async-start(bf16[64,32,128]{2,1,0:T(8,128)(2,1)} %coeffs.1), calls=%async_computation | async-start | bytes 1048576 | tf_op jit(solution)/shard_map/all_to_all | solution.py:314
  17.3 15.7 %copy-start.4 = (s32[1,128,4]{1,2,0:T(4,128)S(1)}, s32[1,128,4]{1,2,0:T(4,128)}, u32[]{:S(2)}) copy-start(s32[1,128,4]{1,2,0:T(4,128)} %param.13) | copy-start | bytes 6148
  17.3 15.7 %copy-start.5 = (bf16[128,64,128]{2,1,0:T(8,128)(2,1)S(1)}, bf16[128,64,128]{2,1,0:T(8,128)(2,1)}, u32[]{:S(2)}) copy-start(bf16[128,64,128]{2,1,0:T(8,128)(2,1)} %constant.11.clone.phi_ref) | copy-start | bytes 6291460
  17.4 15.7 %copy-start.6 = (bf16[256,128]{1,0:T(8,128)(2,1)S(1)}, bf16[256,128]{1,0:T(8,128)(2,1)}, u32[]{:S(2)}) copy-start(bf16[256,128]{1,0:T(8,128)(2,1)} %constant.10.clone.w_ref) | copy-start | bytes 196612
  27.4 0.8 %copy-start.7 = (f32[512,256]{1,0:T(8,128)}, f32[512,256]{1,0:T(8,128)S(1)}, u32[]{:S(2)}) copy-start(f32[512,256]{1,0:T(8,128)S(1)} %get-tuple-element.11.g_hbm) | copy-start | bytes 1572868
  29.2 3.8 %collective-permute-start = (bf16[64,32,128]{2,1,0:T(8,128)(2,1)S(1)}, bf16[64,32,128]{2,1,0:T(8,128)(2,1)S(1)}, u32[]{:S(2)}, u32[]{:S(2)}) collective-permute-start(bf16[64,32,128]{2,1,0:T(8,128)(2,1)S(1)} %all-to-all-done), channel_id=1, source_target_pairs={{0,1},{1,0},{2,3},{3,2},{4,5},{5,4},{6,7},{7,6},{8,9},{9,8},{10,11... | collective-permute-start | bytes 1572872 | tf_op jit(solution)/shard_map/ppermute | solution.py:337
  33.1 1.0 %copy-start.8 = (f32[512,256]{1,0:T(8,128)S(1)}, f32[512,256]{1,0:T(8,128)}, u32[]{:S(2)}) copy-start(f32[512,256]{1,0:T(8,128)} %copy-done.7) | copy-start | bytes 1572868

commit v3 on v2

--- a/solution.py
+++ b/solution.py
@@ -28,7 +28,11 @@
 CHIPS = 64
 PEERS = [[core + 2 * chip for chip in range(CHIPS)] for core in range(2)]
 MIB = 1024 * 1024
-UNROLL = 2
+PAIRS = 64
+SPARE = 32
+FIELDS = 8
+LOOK = 16
+BACK = 4
 NT = (((1,), (1,)), ((), ()))
 
 
@@ -39,7 +43,8 @@
     both = np.concatenate([np.cos(phase), -np.sin(phase)], axis=1)
     both = both.reshape(NPHI, 2, MODES // 2, 2).transpose(0, 1, 3, 2)
     blocks = both.reshape(NPHI // 32, 32, 2 * MODES).transpose(0, 2, 1)
-    return np.tile(blocks, (1, 1, 4)).astype(jnp.bfloat16)
+    tiled = np.tile(blocks, (1, 1, 4))
+    return np.concatenate([tiled, np.zeros_like(tiled[:SPARE])]).astype(jnp.bfloat16)
 
 
 def psi_tables():
@@ -96,7 +101,8 @@
         copy.wait()
 
 
-def bucket_kernel(slot_ref, phi_ref, psi_ref, frac_ref, g_ref, rank_ref, carry, lhs, hot):
+def bucket_kernel(slot_ref, phi_ref, psi_ref, frac_ref, *refs):
+    fields, (ids_ref, pair_ref, lane_ref, g_ref, rank_ref, carry, lhs, hot) = refs[:FIELDS], refs[FIELDS:]
     zero = jnp.zeros((), BF)
     one = jnp.ones((), BF)
     own_iota = iota_bf((OWNERS, LANES), 0)
@@ -140,27 +146,77 @@
 
     lax.fori_loop(0, 16, block, 0, unroll=4)
 
+    square = (OWNERS, OWNERS)
+    across = lax.broadcasted_iota(jnp.int32, square, 1).astype(F32)
+    down = lax.broadcasted_iota(jnp.int32, square, 0).astype(F32)
+    heavy = carry[...] > 128.0
+    earlier = jnp.where(across < down, 1.0, 0.0).astype(BF)
+    ahead = jnp.dot(
+        earlier, jnp.where(heavy, 1.0, 0.0).astype(BF), preferred_element_type=F32
+    )
+    pair = jnp.where(heavy, ahead, down - ahead)
+    here = pair == across
+    first = jnp.where(heavy, jnp.where(here, 1.0, 0.0), 0.0)
+    second = jnp.where(heavy, 0.0, jnp.where(here, 1.0, 0.0))
+    ids_ref[...] = jnp.concatenate(
+        [jnp.sum(pick * down, axis=0, keepdims=True) for pick in (first, second)], axis=0
+    ).astype(jnp.int32)
+    first = first.T[:PAIRS].astype(BF)
+    second = second.T[:PAIRS].astype(BF)
+    late = lax.broadcasted_iota(jnp.int32, (PAIRS, WIDE), 1) >= RANKS
+    merged = []
+    for n in range(ITEMS):
+        values = g_ref[n * OWNERS : (n + 1) * OWNERS, :].astype(BF)
+        long = jnp.dot(first, values, preferred_element_type=F32)
+        short = jnp.dot(second, values, preferred_element_type=F32)
+        merged.append(jnp.where(late, pltpu.roll(short, RANKS, axis=1), long))
+    row, psi, a, b = merged
+    row = jnp.where(late, row + 128.0, row)
+    fields[0][...] = row
+    fields[1][...] = row + 1.0
+    fields[2][...] = psi
+    fields[3][...] = jnp.where(psi == NPSI - 1.0, 0.0, psi + 1.0)
+    fields[4][...] = 1.0 - a
+    fields[5][...] = a
+    fields[6][...] = 1.0 - b
+    fields[7][...] = b
+    lane_ref[...] = jnp.where(heavy, pair, pair + 64.0)
+
+    def address(step, code):
+        start = pl.multiple_of(step * 8, 8)
+        owners = slot_ref[pl.ds(start, 8), :] >> 2
+        found = jnp.concatenate(
+            [
+                jnp.sum(
+                    jnp.where(own_wide == owners[u : u + 1], code[...], 0.0), axis=0, keepdims=True
+                )
+                for u in range(8)
+            ],
+            axis=0,
+        )
+        light = found >= 64.0
+        pair_ref[pl.ds(start, 8), :] = jnp.where(light, found - 64.0, found)
+        rank_ref[pl.ds(start, 8), :] += jnp.where(light, 1.0 * RANKS, 0.0)
+        return code
+
+    carry[...] = lane_ref[...]
+    lax.fori_loop(0, 16, lambda step, _: (address(step, carry), 0)[1], 0, unroll=2)
+    lane_ref[...] = rank_ref[...]
+
 
 def eval_kernel(
     visits_ref,
     core_ref,
+    ids_ref,
     mine_ref,
     theirs_ref,
     w_ref,
     phi_ref,
-    g_hbm,
-    slot_ref,
-    rank_ref,
-    out_ref,
-    coeff,
-    spec,
-    tile_ref,
-    found,
-    g_ref,
-    sem,
+    pair_ref,
+    lane_ref,
+    *refs,
 ):
-    fetch = pltpu.make_async_copy(g_hbm, g_ref, sem)
-    fetch.start()
+    fields, (out_ref, coeff, spec, tile_ref, found) = refs[:FIELDS], refs[FIELDS:]
     zero = jnp.zeros((), BF)
     one = jnp.ones((), BF)
     lane = lax.broadcasted_iota(jnp.int32, (1, LANES), 1) // 32
@@ -218,58 +274,56 @@
                 )
             cells = jnp.dot(source, jnp.concatenate(chosen, axis=1), preferred_element_type=F32)
             for v in range(2):
-                tile_ref[s * 4 + 2 * pair + v] = cells[:, v * LANES : (v + 1) * LANES].astype(BF)
-
-    row_iota = iota_bf((LANES, WIDE), 0)
-
-    def look(s):
-        for o in range(4):
-            d = o * SHARDS + s
-            at = [g_ref[pl.ds(n * OWNERS + d, 1), :] for n in range(ITEMS)]
-            row0 = at[0].astype(BF)
-            row1 = (at[0] + 1.0).astype(BF)
-            q0 = at[1].astype(BF)
-            q1 = jnp.where(at[1] == NPSI - 1.0, 0.0, at[1] + 1.0).astype(BF)
-            a0, a1 = (1.0 - at[2]).astype(BF), at[2].astype(BF)
-            b0, b1 = (1.0 - at[3]).astype(BF), at[3].astype(BF)
-            hot = jnp.where(row_iota == row0, a0, jnp.where(row_iota == row1, a1, zero))
-            seen = jnp.dot(tile_ref[s * 4 + o], hot, preferred_element_type=F32)
-            weight = jnp.where(row_iota == q0, b0, jnp.where(row_iota == q1, b1, zero))
-            found[pl.ds(d, 1), :] = jnp.sum(seen * weight.astype(F32), axis=0, keepdims=True)
-
-    def work(pair, stages):
-        if 2 in stages:
-            for v in range(2):
-                look((pair - 2) * 2 + v)
-        if 1 in stages:
-            for v in range(2):
-                tiles((pair - 1) * 2 + v)
-        if 0 in stages:
-            spectrum(pair)
+                tile_ref[(2 * pair + v) * SHARDS + s] = cells[:, v * LANES : (v + 1) * LANES].astype(BF)
 
     def turn(pair, _):
-        work(pair, (0, 1, 2))
+        for v in range(2):
+            tiles((pair - 1) * 2 + v)
+        spectrum(pair)
         return 0
 
-    work(0, (0,))
-    work(1, (0, 1))
-    fetch.wait()
-    lax.fori_loop(2, SHARDS // 2, turn, 0, unroll=UNROLL)
-    work(SHARDS // 2, (1, 2))
-    work(SHARDS // 2 + 1, (2,))
-
-    rank_iota = iota_bf((RANKS, LANES), 0)
-    own_iota = iota_bf((OWNERS, LANES), 0)
+    spectrum(0)
+    lax.fori_loop(1, SHARDS // 2, turn, 0, unroll=3)
+    for v in range(2):
+        tiles(SHARDS - 2 + v)
+
+    near = iota_bf((LANES, WIDE), 0)
+    far = near[:, LANES:] + jnp.asarray(128.0, BF)
+    empty = jnp.zeros((LANES, LANES), BF)
+
+    def look(step, _):
+        for u in range(LOOK):
+            p = step * LOOK + u
+            row0, row1, q0, q1, a0, a1, b0, b1 = [
+                field[pl.ds(p, 1), :].astype(BF) for field in fields
+            ]
+            top = jnp.where(near == row0, a0, jnp.where(near == row1, a1, zero))
+            low = jnp.where(
+                far == row0[:, LANES:],
+                a0[:, LANES:],
+                jnp.where(far == row1[:, LANES:], a1[:, LANES:], zero),
+            )
+            hot = jnp.concatenate([top, jnp.concatenate([empty, low], axis=1)], axis=0)
+            both = jnp.concatenate([tile_ref[ids_ref[0, p]], tile_ref[ids_ref[1, p]]], axis=1)
+            seen = jnp.dot(both, hot, preferred_element_type=F32)
+            weight = jnp.where(near == q0, b0, jnp.where(near == q1, b1, zero))
+            found[pl.ds(p, 1), :] = jnp.sum(seen * weight.astype(F32), axis=0, keepdims=True)
+        return 0
+
+    lax.fori_loop(0, PAIRS // LOOK, look, 0)
+
+    lane_iota = iota_bf((WIDE, LANES), 0)
+    pair_iota = iota_bf((PAIRS, LANES), 0)
 
     def back(step, values):
         start = pl.multiple_of(step * 8, 8)
-        owners = (slot_ref[pl.ds(start, 8), :] >> 2).astype(F32)
-        ranks = rank_ref[pl.ds(start, 8), :]
+        pairs = pair_ref[pl.ds(start, 8), :]
+        lanes = lane_ref[pl.ds(start, 8), :]
         result = []
         for u in range(0, 8, 2):
             hot = jnp.concatenate(
                 [
-                    jnp.where(rank_iota == ranks[v : v + 1].astype(BF), one, zero)
+                    jnp.where(lane_iota == lanes[v : v + 1].astype(BF), one, zero)
                     for v in (u, u + 1)
                 ],
                 axis=1,
@@ -277,12 +331,14 @@
             moved = jnp.dot(values, hot, preferred_element_type=F32).astype(BF)
             for v in (u, u + 1):
                 part = moved[:, (v - u) * LANES : (v - u + 1) * LANES]
-                part = jnp.where(own_iota == owners[v : v + 1].astype(BF), part, zero)
-                result.append(jnp.sum(part.astype(F32), axis=0, keepdims=True))
+                part = jnp.where(pair_iota == pairs[v : v + 1].astype(BF), part, zero)
+                part = part[:32] + part[32:]
+                part = (part[:16] + part[16:]).astype(F32)
+                result.append(jnp.sum(part, axis=0, keepdims=True))
         out_ref[pl.ds(start, 8), :] = jnp.concatenate(result, axis=0)
         return values
 
-    lax.fori_loop(0, 16, back, found[...][:, :RANKS].astype(BF), unroll=4)
+    lax.fori_loop(0, 16, back, found[...].astype(BF), unroll=BACK)
 
 
 def shards(sky_coeffs, beam_coeffs, wigner, visits, point_slot, phi_cell, psi_cell, fraction):
@@ -314,15 +370,16 @@
     mine = lax.all_to_all(copies, MESH_AXES, 0, 0, axis_index_groups=PEERS, tiled=True)
     core = jnp.full((1,), lax.axis_index("shard") & 1, jnp.int32)
     slots = point_slot.reshape(OWNERS, LANES)
-    grouped, ranks = pl.pallas_call(
+    table = jax.ShapeDtypeStruct((OWNERS, LANES), F32)
+    *fields, ids, pairs, lanes = pl.pallas_call(
         bucket_kernel,
-        out_shape=(
-            jax.ShapeDtypeStruct((ITEMS * OWNERS, WIDE), F32),
-            jax.ShapeDtypeStruct((OWNERS, LANES), F32),
-        ),
+        out_shape=[jax.ShapeDtypeStruct((PAIRS, WIDE), F32)] * FIELDS
+        + [jax.ShapeDtypeStruct((2, OWNERS), jnp.int32), table, table],
         in_specs=[vmem] * 4,
-        out_specs=(vmem, vmem),
+        out_specs=[vmem] * (FIELDS + 3),
         scratch_shapes=[
+            pltpu.VMEM((ITEMS * OWNERS, WIDE), F32),
+            pltpu.VMEM((OWNERS, LANES), F32),
             pltpu.VMEM((OWNERS, LANES), F32),
             pltpu.VMEM((ITEMS * OWNERS, 8 * LANES), BF),
             pltpu.VMEM((RANKS, 8 * LANES), BF),
@@ -333,20 +390,18 @@
         ),
         name="bucket",
     )(slots, phi_cell.reshape(OWNERS, LANES), psi_cell.reshape(OWNERS, LANES), fraction)
-    mine, ranks = lax.optimization_barrier((mine, ranks))
+    mine, lanes = lax.optimization_barrier((mine, lanes))
     theirs = lax.ppermute(mine, "shard", [(n, n ^ 1) for n in range(SHARDS)])
     timeline = pl.pallas_call(
         eval_kernel,
         out_shape=jax.ShapeDtypeStruct((OWNERS, LANES), F32),
-        in_specs=[pl.BlockSpec(memory_space=pltpu.SMEM)] * 2 + [vmem] * 4 + [anywhere] + [vmem] * 2,
+        in_specs=[pl.BlockSpec(memory_space=pltpu.SMEM)] * 3 + [vmem] * (6 + FIELDS),
         out_specs=vmem,
         scratch_shapes=[
             pltpu.VMEM((OWNERS * SHARDS, LANES), F32),
             pltpu.VMEM((SHARDS, NPSI, 2 * LANES), BF),
             pltpu.VMEM((OWNERS, NPSI, LANES), BF),
-            pltpu.VMEM((OWNERS, WIDE), F32),
-            pltpu.VMEM((ITEMS * OWNERS, WIDE), F32),
-            dma,
+            pltpu.VMEM((PAIRS, WIDE), F32),
         ],
         compiler_params=pltpu.CompilerParams(vmem_limit_bytes=24 * MIB),
         cost_estimate=pl.CostEstimate(
@@ -356,13 +411,14 @@
     )(
         visits[0].T,
         core,
+        ids,
         mine.reshape(CHIPS * SHARDS, LANES),
         theirs.reshape(CHIPS * SHARDS, LANES),
         jnp.asarray(psi_tables()),
         jnp.asarray(phi_tables()),
-        grouped,
-        slots,
-        ranks,
+        pairs,
+        lanes,
+        *fields,
     )
     return timeline.reshape(-1)
 

time: 48.1 us -> 46.9 us (0.975)
  waiting for transfers between devices: 2.6 us -> 1.72 us
    pallas_call x1, Pallas kernels: 13.8 us -> 11.9 us  [shards(): pl.pallas_call(eval_kernel, out_shape=jax.ShapeDtypeStruct((OWNERS, LANES...]
    pallas_call x1, Pallas kernels: 9.98 us -> 11.7 us  [shards(): pl.pallas_call(bucket_kernel, out_shape=[jax.ShapeDtypeStruct((PAIRS, WID...]
    all_to_all x1, waiting for transfers between devices: 1.07 us -> 0.18 us  [shards(): lax.all_to_all(copies, MESH_AXES, 0, 0, axis_index_groups=PEERS, tiled=True)]
    unnamed x18 -> x14, local copies, waits for them, and re-layouts: 1.87 us -> 1.77 us
  transfers between devices with their start and end apart: 2 -> 2, of which waited for: 2 -> 2; matrix products, arithmetic and copies ran while one was open for 0% -> 0% of each run, Pallas kernels for 21% -> 25%
where the time goes in v3:
time: 46.9 us; the launch traced here: 46.7 us
  Pallas kernels  28.9 us (62%)
  starting transfers between devices  14.3 us (30%)
  local copies, waits for them, and re-layouts  1.77 us (4%)
  waiting for transfers between devices  1.72 us (4%)
    all_to_all x1, starting transfers between devices, shards(): lax.all_to_all(copies, MESH_AXES, 0, 0, axis_index_groups=PEERS, tiled=True)  12 us
    pallas_call x1, Pallas kernels, shards(): pl.pallas_call(eval_kernel, out_shape=jax.ShapeDtypeStruct((OWNERS, LANES...  11.9 us
    pallas_call x1, Pallas kernels, shards(): pl.pallas_call(bucket_kernel, out_shape=[jax.ShapeDtypeStruct((PAIRS, WID...  11.7 us
    pallas_call x1, Pallas kernels, shards(): pl.pallas_call(coeff_kernel, out_shape=jax.ShapeDtypeStruct((CHIPS, SHARD...  5.28 us
    ppermute x1, starting transfers between devices, shards(): theirs = lax.ppermute(mine, 'shard', [(n, n ^ 1) for n in range(SHARDS)])  2.29 us
    unnamed x14, local copies, waits for them, and re-layouts  1.77 us
    ppermute x1, waiting for transfers between devices, shards(): theirs = lax.ppermute(mine, 'shard', [(n, n ^ 1) for n in range(SHARDS)])  1.54 us
  transfers between devices with their start and end apart: 2, of which 2 were waited for; matrix products, arithmetic and copies ran while one was open for 0% of the time, Pallas kernels for 25%

profile of v3, /device:TPU:1, one launch (start us, length us, event | category | flops | bytes accessed | tf_op | source)
XLA Modules:
  0.0 46.7 jit_solution(17214261043431753148)
XLA Ops:
  0.0 0.0 copy-start
  0.0 0.0 copy-start.3
  0.0 0.0 copy-start.2
  0.0 0.0 copy-start.1
  0.0 5.3 %coeffs.1 = bf16[64,32,128]{2,1,0:T(8,128)(2,1)} custom-call(f32[1,2,2048]{2,1,0:T(2,128)} %sky_hbm.1, f32[16,2048]{1,0:T(8,128)} %beam_hbm.1, bf16[1,16,2048,128]{3,2,1,0:T(8,128)(2,1)} %wigner_hbm.1), custom_call_target="tpu_custom_call" | custom-call | flops 16777216 | bytes 9437184 | tf_op jit(solution)/shard_map/coeffs/pallas_call | solution.py:348
  5.3 12.0 %all-to-all-start = ((bf16[64,32,128]{2,1,0:T(8,128)(2,1)}), bf16[64,32,128]{2,1,0:T(8,128)(2,1)S(1)}, u32[]{:S(2)}, u32[]{:S(2)}) async-start(bf16[64,32,128]{2,1,0:T(8,128)(2,1)} %coeffs.1), calls=%async_computation | async-start | bytes 1048576 | tf_op jit(solution)/shard_map/all_to_all | solution.py:370
  17.3 0.0 copy-done
  17.3 0.0 copy-done.3
  17.3 0.0 copy-done.2
  17.3 0.0 copy-done.1
  17.3 0.0 copy-start.4
  17.3 0.0 copy-start.6
  17.4 11.7 %bucket.1 = (f32[64,256]{1,0:T(8,128)S(1)}, f32[64,256]{1,0:T(8,128)S(1)}, f32[64,256]{1,0:T(8,128)S(1)}, f32[64,256]{1,0:T(8,128)S(1)}, f32[64,256]{1,0:T(8,128...) custom-call(s32[128,128]{1,0:T(8,128)S(1)} %bitcast.12, ...), custom_call_target="tpu_custom_call" | custom-call | flops 8589934592 | bytes 2097152 | tf_op jit(solution)/shard_map/bucket/pallas_call | solution.py:374
  29.1 0.2 all-to-all-done
  29.2 2.3 %collective-permute-start = (bf16[64,32,128]{2,1,0:T(8,128)(2,1)S(1)}, bf16[64,32,128]{2,1,0:T(8,128)(2,1)S(1)}, u32[]{:S(2)}, u32[]{:S(2)}) collective-permute-start(bf16[64,32,128]{2,1,0:T(8,128)(2,1)S(1)} %all-to-all-done), channel_id=1, source_target_pairs={{0,1},{1,0},{2,3},{3,2},{4,5},{5,4},{6,7},{7,6},{8,9},{9,8},{10,11... | collective-permute-start | bytes 1572872 | tf_op jit(solution)/shard_map/ppermute | solution.py:394
  31.5 1.5 %collective-permute-done = bf16[64,32,128]{2,1,0:T(8,128)(2,1)S(1)} collective-permute-done((bf16[64,32,128]{2,1,0:T(8,128)(2,1)S(1)}, bf16[64,32,128]{2,1,0:T(8,128)(2,1)S(1)}, u32[]{:S(2)}, u32[]{:S(2)}) %collective-permute-start) | collective-permute-done | bytes 524320 | tf_op jit(solution)/shard_map/ppermute | solution.py:394
  33.1 0.0 copy-done.4
  33.1 0.0 copy-done.6
  33.1 0.0 copy-start.5
  33.1 1.7 %copy-done.5 = bf16[160,64,128]{2,1,0:T(8,128)(2,1)S(1)} copy-done((bf16[160,64,128]{2,1,0:T(8,128)(2,1)S(1)}, bf16[160,64,128]{2,1,0:T(8,128)(2,1)}, u32[]{:S(2)}) %copy-start.5) | copy-done | bytes 2621464
  34.8 11.9 %evaluate.1 = f32[128,128]{1,0:T(8,128)} custom-call(s32[4,128]{1,0:T(4,128)S(1)} %bitcast.15, s32[1]{0:T(128)} %bitcast.2.core_ref, s32[2,128]{1,0:T(2,128)S(1)} %get-tuple-element.18.ids_ref, bf16[2048,128]{1,0:T(8,128)(2,1)S(1)} %bitcast.10, bf16[2048,128]{1,0:T(8,128)(2,1)S(1)} %bitcast.11, bf16[256,128]{1,0:T(8,128)(2,1)S(1)} %copy-done.6, ...), custom_call_target="tpu_custom_call" | custom-call | flops 8589934592 | bytes 4194304 | tf_op jit(solution)/shard_map/evaluate/pallas_call | solution.py:395
Async XLA Ops:
  0.0 17.3 %copy-start = (f32[2,16384]{1,0:T(2,128)S(1)}, f32[2,16384]{1,0:T(2,128)}, u32[]{:S(2)}) copy-start(f32[2,16384]{1,0:T(2,128)} %frac_ref.1) | copy-start | bytes 393220
  0.0 17.3 %copy-start.3 = (s32[16384]{0:T(1024)S(1)}, s32[16384]{0:T(1024)}, u32[]{:S(2)}) copy-start(s32[16384]{0:T(1024)} %param.16) | copy-start | bytes 196612
  0.0 17.3 %copy-start.2 = (s32[16384]{0:T(1024)S(1)}, s32[16384]{0:T(1024)}, u32[]{:S(2)}) copy-start(s32[16384]{0:T(1024)} %param.15) | copy-start | bytes 196612
  0.0 17.3 %copy-start.1 = (s32[16384]{0:T(1024)S(1)}, s32[16384]{0:T(1024)}, u32[]{:S(2)}) copy-start(s32[16384]{0:T(1024)} %param.14) | copy-start | bytes 196612
  5.3 23.9 %all-to-all-start = ((bf16[64,32,128]{2,1,0:T(8,128)(2,1)}), bf16[64,32,128]{2,1,0:T(8,128)(2,1)S(1)}, u32[]{:S(2)}, u32[]{:S(2)}) async-start(bf16[64,32,128]{2,1,0:T(8,128)(2,1)} %coeffs.1), calls=%async_computation | async-start | bytes 1048576 | tf_op jit(solution)/shard_map/all_to_all | solution.py:370
  17.3 15.7 %copy-start.4 = (s32[1,128,4]{1,2,0:T(4,128)S(1)}, s32[1,128,4]{1,2,0:T(4,128)}, u32[]{:S(2)}) copy-start(s32[1,128,4]{1,2,0:T(4,128)} %param.13) | copy-start | bytes 6148
  17.3 15.7 %copy-start.6 = (bf16[256,128]{1,0:T(8,128)(2,1)S(1)}, bf16[256,128]{1,0:T(8,128)(2,1)}, u32[]{:S(2)}) copy-start(bf16[256,128]{1,0:T(8,128)(2,1)} %constant.10.clone.w_ref) | copy-start | bytes 196612
  29.2 3.8 %collective-permute-start = (bf16[64,32,128]{2,1,0:T(8,128)(2,1)S(1)}, bf16[64,32,128]{2,1,0:T(8,128)(2,1)S(1)}, u32[]{:S(2)}, u32[]{:S(2)}) collective-permute-start(bf16[64,32,128]{2,1,0:T(8,128)(2,1)S(1)} %all-to-all-done), channel_id=1, source_target_pairs={{0,1},{1,0},{2,3},{3,2},{4,5},{5,4},{6,7},{7,6},{8,9},{9,8},{10,11... | collective-permute-start | bytes 1572872 | tf_op jit(solution)/shard_map/ppermute | solution.py:394
  33.1 1.7 %copy-start.5 = (bf16[160,64,128]{2,1,0:T(8,128)(2,1)S(1)}, bf16[160,64,128]{2,1,0:T(8,128)(2,1)}, u32[]{:S(2)}) copy-start(bf16[160,64,128]{2,1,0:T(8,128)(2,1)} %constant.11.clone.phi_ref) | copy-start | bytes 7864324

commit v4 on v3

--- a/solution.py
+++ b/solution.py
@@ -29,7 +29,6 @@
 PEERS = [[core + 2 * chip for chip in range(CHIPS)] for core in range(2)]
 MIB = 1024 * 1024
 PAIRS = 64
-SPARE = 32
 FIELDS = 8
 LOOK = 16
 BACK = 4
@@ -42,9 +41,8 @@
     phase = ((phi * mode) % NPHI).astype(np.float64) * (2.0 * math.pi / NPHI)
     both = np.concatenate([np.cos(phase), -np.sin(phase)], axis=1)
     both = both.reshape(NPHI, 2, MODES // 2, 2).transpose(0, 1, 3, 2)
-    blocks = both.reshape(NPHI // 32, 32, 2 * MODES).transpose(0, 2, 1)
-    tiled = np.tile(blocks, (1, 1, 4))
-    return np.concatenate([tiled, np.zeros_like(tiled[:SPARE])]).astype(jnp.bfloat16)
+    blocks = both.reshape(NPHI // LANES, LANES, 2 * MODES).transpose(0, 2, 1)
+    return blocks.astype(jnp.bfloat16)
 
 
 def psi_tables():
@@ -258,7 +256,8 @@
                 waves, lane_row = None, None
                 for j in range(4):
                     tile = jnp.maximum(visits_ref[j, o * SHARDS + s], 0)
-                    wave = phi_ref[o * 32 + (tile & 31)]
+                    turn_by = ((j - tile) & 3) * 32
+                    wave = pltpu.roll(phi_ref[o * 8 + ((tile & 31) >> 2)], turn_by, axis=1)
                     row = jnp.full((1, LANES), tile >> 5, jnp.int32)
                     waves = wave if j == 0 else jnp.where(lane == j, wave, waves)
                     lane_row = row if j == 0 else jnp.where(lane == j, row, lane_row)

time: 46.9 us -> 45.9 us (0.979)
  local copies, waits for them, and re-layouts: 1.77 us -> 0.04 us
  Pallas kernels: 28.9 us -> 29.7 us
    unnamed x14, local copies, waits for them, and re-layouts: 1.77 us -> 0.04 us
    pallas_call x1, Pallas kernels: 11.9 us -> 12.7 us  [shards(): pl.pallas_call(eval_kernel, out_shape=jax.ShapeDtypeStruct((OWNERS, LANES...]
  transfers between devices with their start and end apart: 2 -> 2, of which waited for: 2 -> 2; matrix products, arithmetic and copies ran while one was open for 0% -> 0% of each run, Pallas kernels for 25% -> 26%
where the time goes in v4:
time: 45.9 us; the launch traced here: 45.8 us
  Pallas kernels  29.7 us (65%)
  starting transfers between devices  14.3 us (31%)
  waiting for transfers between devices  1.7 us (4%)
    pallas_call x1, Pallas kernels, shards(): pl.pallas_call(eval_kernel, out_shape=jax.ShapeDtypeStruct((OWNERS, LANES...  12.7 us
    all_to_all x1, starting transfers between devices, shards(): lax.all_to_all(copies, MESH_AXES, 0, 0, axis_index_groups=PEERS, tiled=True)  12 us
    pallas_call x1, Pallas kernels, shards(): pl.pallas_call(bucket_kernel, out_shape=[jax.ShapeDtypeStruct((PAIRS, WID...  11.7 us
    pallas_call x1, Pallas kernels, shards(): pl.pallas_call(coeff_kernel, out_shape=jax.ShapeDtypeStruct((CHIPS, SHARD...  5.28 us
    ppermute x1, starting transfers between devices, shards(): theirs = lax.ppermute(mine, 'shard', [(n, n ^ 1) for n in range(SHARDS)])  2.29 us
    ppermute x1, waiting for transfers between devices, shards(): theirs = lax.ppermute(mine, 'shard', [(n, n ^ 1) for n in range(SHARDS)])  1.54 us
  transfers between devices with their start and end apart: 2, of which 2 were waited for; matrix products, arithmetic and copies ran while one was open for 0% of the time, Pallas kernels for 26%

profile of v4, /device:TPU:1, one launch (start us, length us, event | category | flops | bytes accessed | tf_op | source)
XLA Modules:
  0.0 45.8 jit_solution(5788803397961003862)
XLA Ops:
  0.0 0.0 copy-start
  0.0 0.0 copy-start.3
  0.0 0.0 copy-start.2
  0.0 0.0 copy-start.1
  0.0 5.3 %coeffs.1 = bf16[64,32,128]{2,1,0:T(8,128)(2,1)} custom-call(f32[1,2,2048]{2,1,0:T(2,128)} %sky_hbm.1, f32[16,2048]{1,0:T(8,128)} %beam_hbm.1, bf16[1,16,2048,128]{3,2,1,0:T(8,128)(2,1)} %wigner_hbm.1), custom_call_target="tpu_custom_call" | custom-call | flops 16777216 | bytes 9437184 | tf_op jit(solution)/shard_map/coeffs/pallas_call | solution.py:347
  5.3 12.0 %all-to-all-start = ((bf16[64,32,128]{2,1,0:T(8,128)(2,1)}), bf16[64,32,128]{2,1,0:T(8,128)(2,1)S(1)}, u32[]{:S(2)}, u32[]{:S(2)}) async-start(bf16[64,32,128]{2,1,0:T(8,128)(2,1)} %coeffs.1), calls=%async_computation | async-start | bytes 1048576 | tf_op jit(solution)/shard_map/all_to_all | solution.py:369
  17.3 0.0 copy-done
  17.3 0.0 copy-done.3
  17.3 0.0 copy-done.2
  17.3 0.0 copy-done.1
  17.3 0.0 copy-start.4
  17.3 0.0 copy-start.5
  17.4 0.0 copy-start.6
  17.4 11.7 %bucket.1 = (f32[64,256]{1,0:T(8,128)S(1)}, f32[64,256]{1,0:T(8,128)S(1)}, f32[64,256]{1,0:T(8,128)S(1)}, f32[64,256]{1,0:T(8,128)S(1)}, f32[64,256]{1,0:T(8,128...) custom-call(s32[128,128]{1,0:T(8,128)S(1)} %bitcast.12, ...), custom_call_target="tpu_custom_call" | custom-call | flops 8589934592 | bytes 2097152 | tf_op jit(solution)/shard_map/bucket/pallas_call | solution.py:373
  29.1 0.2 all-to-all-done
  29.2 2.3 %collective-permute-start = (bf16[64,32,128]{2,1,0:T(8,128)(2,1)S(1)}, bf16[64,32,128]{2,1,0:T(8,128)(2,1)S(1)}, u32[]{:S(2)}, u32[]{:S(2)}) collective-permute-start(bf16[64,32,128]{2,1,0:T(8,128)(2,1)S(1)} %all-to-all-done), channel_id=1, source_target_pairs={{0,1},{1,0},{2,3},{3,2},{4,5},{5,4},{6,7},{7,6},{8,9},{9,8},{10,11... | collective-permute-start | bytes 1572872 | tf_op jit(solution)/shard_map/ppermute | solution.py:393
  31.5 1.5 %collective-permute-done = bf16[64,32,128]{2,1,0:T(8,128)(2,1)S(1)} collective-permute-done((bf16[64,32,128]{2,1,0:T(8,128)(2,1)S(1)}, bf16[64,32,128]{2,1,0:T(8,128)(2,1)S(1)}, u32[]{:S(2)}, u32[]{:S(2)}) %collective-permute-start) | collective-permute-done | bytes 524320 | tf_op jit(solution)/shard_map/ppermute | solution.py:393
  33.1 0.0 copy-done.4
  33.1 0.0 copy-done.5
  33.1 0.0 copy-done.6
  33.1 12.7 %evaluate.1 = f32[128,128]{1,0:T(8,128)} custom-call(s32[4,128]{1,0:T(4,128)S(1)} %bitcast.15, s32[1]{0:T(128)} %bitcast.2.core_ref, s32[2,128]{1,0:T(2,128)S(1)} %get-tuple-element.18.ids_ref, bf16[2048,128]{1,0:T(8,128)(2,1)S(1)} %bitcast.10, bf16[2048,128]{1,0:T(8,128)(2,1)S(1)} %bitcast.11, bf16[256,128]{1,0:T(8,128)(2,1)S(1)} %copy-done.6, ...), custom_call_target="tpu_custom_call" | custom-call | flops 8589934592 | bytes 4194304 | tf_op jit(solution)/shard_map/evaluate/pallas_call | solution.py:394
Async XLA Ops:
  0.0 17.3 %copy-start = (f32[2,16384]{1,0:T(2,128)S(1)}, f32[2,16384]{1,0:T(2,128)}, u32[]{:S(2)}) copy-start(f32[2,16384]{1,0:T(2,128)} %frac_ref.1) | copy-start | bytes 393220
  0.0 17.3 %copy-start.3 = (s32[16384]{0:T(1024)S(1)}, s32[16384]{0:T(1024)}, u32[]{:S(2)}) copy-start(s32[16384]{0:T(1024)} %param.16) | copy-start | bytes 196612
  0.0 17.3 %copy-start.2 = (s32[16384]{0:T(1024)S(1)}, s32[16384]{0:T(1024)}, u32[]{:S(2)}) copy-start(s32[16384]{0:T(1024)} %param.15) | copy-start | bytes 196612
  0.0 17.3 %copy-start.1 = (s32[16384]{0:T(1024)S(1)}, s32[16384]{0:T(1024)}, u32[]{:S(2)}) copy-start(s32[16384]{0:T(1024)} %param.14) | copy-start | bytes 196612
  5.3 23.9 %all-to-all-start = ((bf16[64,32,128]{2,1,0:T(8,128)(2,1)}), bf16[64,32,128]{2,1,0:T(8,128)(2,1)S(1)}, u32[]{:S(2)}, u32[]{:S(2)}) async-start(bf16[64,32,128]{2,1,0:T(8,128)(2,1)} %coeffs.1), calls=%async_computation | async-start | bytes 1048576 | tf_op jit(solution)/shard_map/all_to_all | solution.py:369
  17.3 15.7 %copy-start.4 = (s32[1,128,4]{1,2,0:T(4,128)S(1)}, s32[1,128,4]{1,2,0:T(4,128)}, u32[]{:S(2)}) copy-start(s32[1,128,4]{1,2,0:T(4,128)} %param.13) | copy-start | bytes 6148
  17.3 15.7 %copy-start.5 = (bf16[32,64,128]{2,1,0:T(8,128)(2,1)S(1)}, bf16[32,64,128]{2,1,0:T(8,128)(2,1)}, u32[]{:S(2)}) copy-start(bf16[32,64,128]{2,1,0:T(8,128)(2,1)} %constant.11.clone.phi_ref) | copy-start | bytes 1572868
  17.4 15.7 %copy-start.6 = (bf16[256,128]{1,0:T(8,128)(2,1)S(1)}, bf16[256,128]{1,0:T(8,128)(2,1)}, u32[]{:S(2)}) copy-start(bf16[256,128]{1,0:T(8,128)(2,1)} %constant.10.clone.w_ref) | copy-start | bytes 196612
  29.2 3.8 %collective-permute-start = (bf16[64,32,128]{2,1,0:T(8,128)(2,1)S(1)}, bf16[64,32,128]{2,1,0:T(8,128)(2,1)S(1)}, u32[]{:S(2)}, u32[]{:S(2)}) collective-permute-start(bf16[64,32,128]{2,1,0:T(8,128)(2,1)S(1)} %all-to-all-done), channel_id=1, source_target_pairs={{0,1},{1,0},{2,3},{3,2},{4,5},{5,4},{6,7},{7,6},{8,9},{9,8},{10,11... | collective-permute-start | bytes 1572872 | tf_op jit(solution)/shard_map/ppermute | solution.py:393

commit v5 on v4

--- a/solution.py
+++ b/solution.py
@@ -31,7 +31,7 @@
 PAIRS = 64
 FIELDS = 8
 LOOK = 16
-BACK = 4
+BACK = 8
 NT = (((1,), (1,)), ((), ()))
 
 
@@ -282,7 +282,7 @@
         return 0
 
     spectrum(0)
-    lax.fori_loop(1, SHARDS // 2, turn, 0, unroll=3)
+    lax.fori_loop(1, SHARDS // 2, turn, 0, unroll=15)
     for v in range(2):
         tiles(SHARDS - 2 + v)
 

time: 45.9 us -> 44.5 us (0.969)
  Pallas kernels: 29.7 us -> 28.2 us
    pallas_call x1, Pallas kernels: 12.7 us -> 11.3 us  [shards(): pl.pallas_call(eval_kernel, out_shape=jax.ShapeDtypeStruct((OWNERS, LANES...]
where the time goes in v5:
time: 44.5 us; the launch traced here: 44.3 us
  Pallas kernels  28.2 us (63%)
  starting transfers between devices  14.3 us (32%)
  waiting for transfers between devices  1.7 us (4%)
    all_to_all x1, starting transfers between devices, shards(): lax.all_to_all(copies, MESH_AXES, 0, 0, axis_index_groups=PEERS, tiled=True)  12 us
    pallas_call x1, Pallas kernels, shards(): pl.pallas_call(bucket_kernel, out_shape=[jax.ShapeDtypeStruct((PAIRS, WID...  11.7 us
    pallas_call x1, Pallas kernels, shards(): pl.pallas_call(eval_kernel, out_shape=jax.ShapeDtypeStruct((OWNERS, LANES...  11.3 us
    pallas_call x1, Pallas kernels, shards(): pl.pallas_call(coeff_kernel, out_shape=jax.ShapeDtypeStruct((CHIPS, SHARD...  5.28 us
    ppermute x1, starting transfers between devices, shards(): theirs = lax.ppermute(mine, 'shard', [(n, n ^ 1) for n in range(SHARDS)])  2.29 us
    ppermute x1, waiting for transfers between devices, shards(): theirs = lax.ppermute(mine, 'shard', [(n, n ^ 1) for n in range(SHARDS)])  1.54 us
  transfers between devices with their start and end apart: 2, of which 2 were waited for; matrix products, arithmetic and copies ran while one was open for 0% of the time, Pallas kernels for 26%

profile of v5, /device:TPU:1, one launch (start us, length us, event | category | flops | bytes accessed | tf_op | source)
XLA Modules:
  0.0 44.3 jit_solution(14622607568966455598)
XLA Ops:
  0.0 0.0 copy-start
  0.0 0.0 copy-start.3
  0.0 0.0 copy-start.2
  0.0 0.0 copy-start.1
  0.0 5.3 %coeffs.1 = bf16[64,32,128]{2,1,0:T(8,128)(2,1)} custom-call(f32[1,2,2048]{2,1,0:T(2,128)} %sky_hbm.1, f32[16,2048]{1,0:T(8,128)} %beam_hbm.1, bf16[1,16,2048,128]{3,2,1,0:T(8,128)(2,1)} %wigner_hbm.1), custom_call_target="tpu_custom_call" | custom-call | flops 16777216 | bytes 9437184 | tf_op jit(solution)/shard_map/coeffs/pallas_call | solution.py:347
  5.3 12.0 %all-to-all-start = ((bf16[64,32,128]{2,1,0:T(8,128)(2,1)}), bf16[64,32,128]{2,1,0:T(8,128)(2,1)S(1)}, u32[]{:S(2)}, u32[]{:S(2)}) async-start(bf16[64,32,128]{2,1,0:T(8,128)(2,1)} %coeffs.1), calls=%async_computation | async-start | bytes 1048576 | tf_op jit(solution)/shard_map/all_to_all | solution.py:369
  17.3 0.0 copy-done
  17.3 0.0 copy-done.3
  17.3 0.0 copy-done.2
  17.3 0.0 copy-done.1
  17.3 0.0 copy-start.4
  17.3 0.0 copy-start.5
  17.4 0.0 copy-start.6
  17.4 11.7 %bucket.1 = (f32[64,256]{1,0:T(8,128)S(1)}, f32[64,256]{1,0:T(8,128)S(1)}, f32[64,256]{1,0:T(8,128)S(1)}, f32[64,256]{1,0:T(8,128)S(1)}, f32[64,256]{1,0:T(8,128...) custom-call(s32[128,128]{1,0:T(8,128)S(1)} %bitcast.12, ...), custom_call_target="tpu_custom_call" | custom-call | flops 8589934592 | bytes 2097152 | tf_op jit(solution)/shard_map/bucket/pallas_call | solution.py:373
  29.1 0.2 all-to-all-done
  29.2 2.3 %collective-permute-start = (bf16[64,32,128]{2,1,0:T(8,128)(2,1)S(1)}, bf16[64,32,128]{2,1,0:T(8,128)(2,1)S(1)}, u32[]{:S(2)}, u32[]{:S(2)}) collective-permute-start(bf16[64,32,128]{2,1,0:T(8,128)(2,1)S(1)} %all-to-all-done), channel_id=1, source_target_pairs={{0,1},{1,0},{2,3},{3,2},{4,5},{5,4},{6,7},{7,6},{8,9},{9,8},{10,11... | collective-permute-start | bytes 1572872 | tf_op jit(solution)/shard_map/ppermute | solution.py:393
  31.5 1.5 %collective-permute-done = bf16[64,32,128]{2,1,0:T(8,128)(2,1)S(1)} collective-permute-done((bf16[64,32,128]{2,1,0:T(8,128)(2,1)S(1)}, bf16[64,32,128]{2,1,0:T(8,128)(2,1)S(1)}, u32[]{:S(2)}, u32[]{:S(2)}) %collective-permute-start) | collective-permute-done | bytes 524320 | tf_op jit(solution)/shard_map/ppermute | solution.py:393
  33.1 0.0 copy-done.4
  33.1 0.0 copy-done.5
  33.1 0.0 copy-done.6
  33.1 11.3 %evaluate.1 = f32[128,128]{1,0:T(8,128)} custom-call(s32[4,128]{1,0:T(4,128)S(1)} %bitcast.15, s32[1]{0:T(128)} %bitcast.2.core_ref, s32[2,128]{1,0:T(2,128)S(1)} %get-tuple-element.18.ids_ref, bf16[2048,128]{1,0:T(8,128)(2,1)S(1)} %bitcast.10, bf16[2048,128]{1,0:T(8,128)(2,1)S(1)} %bitcast.11, bf16[256,128]{1,0:T(8,128)(2,1)S(1)} %copy-done.6, ...), custom_call_target="tpu_custom_call" | custom-call | flops 8589934592 | bytes 4194304 | tf_op jit(solution)/shard_map/evaluate/pallas_call | solution.py:394
Async XLA Ops:
  0.0 17.3 %copy-start = (f32[2,16384]{1,0:T(2,128)S(1)}, f32[2,16384]{1,0:T(2,128)}, u32[]{:S(2)}) copy-start(f32[2,16384]{1,0:T(2,128)} %frac_ref.1) | copy-start | bytes 393220
  0.0 17.3 %copy-start.3 = (s32[16384]{0:T(1024)S(1)}, s32[16384]{0:T(1024)}, u32[]{:S(2)}) copy-start(s32[16384]{0:T(1024)} %param.16) | copy-start | bytes 196612
  0.0 17.3 %copy-start.2 = (s32[16384]{0:T(1024)S(1)}, s32[16384]{0:T(1024)}, u32[]{:S(2)}) copy-start(s32[16384]{0:T(1024)} %param.15) | copy-start | bytes 196612
  0.0 17.3 %copy-start.1 = (s32[16384]{0:T(1024)S(1)}, s32[16384]{0:T(1024)}, u32[]{:S(2)}) copy-start(s32[16384]{0:T(1024)} %param.14) | copy-start | bytes 196612
  5.3 23.9 %all-to-all-start = ((bf16[64,32,128]{2,1,0:T(8,128)(2,1)}), bf16[64,32,128]{2,1,0:T(8,128)(2,1)S(1)}, u32[]{:S(2)}, u32[]{:S(2)}) async-start(bf16[64,32,128]{2,1,0:T(8,128)(2,1)} %coeffs.1), calls=%async_computation | async-start | bytes 1048576 | tf_op jit(solution)/shard_map/all_to_all | solution.py:369
  17.3 15.7 %copy-start.4 = (s32[1,128,4]{1,2,0:T(4,128)S(1)}, s32[1,128,4]{1,2,0:T(4,128)}, u32[]{:S(2)}) copy-start(s32[1,128,4]{1,2,0:T(4,128)} %param.13) | copy-start | bytes 6148
  17.3 15.7 %copy-start.5 = (bf16[32,64,128]{2,1,0:T(8,128)(2,1)S(1)}, bf16[32,64,128]{2,1,0:T(8,128)(2,1)}, u32[]{:S(2)}) copy-start(bf16[32,64,128]{2,1,0:T(8,128)(2,1)} %constant.11.clone.phi_ref) | copy-start | bytes 1572868
  17.4 15.7 %copy-start.6 = (bf16[256,128]{1,0:T(8,128)(2,1)S(1)}, bf16[256,128]{1,0:T(8,128)(2,1)}, u32[]{:S(2)}) copy-start(bf16[256,128]{1,0:T(8,128)(2,1)} %constant.10.clone.w_ref) | copy-start | bytes 196612
  29.2 3.8 %collective-permute-start = (bf16[64,32,128]{2,1,0:T(8,128)(2,1)S(1)}, bf16[64,32,128]{2,1,0:T(8,128)(2,1)S(1)}, u32[]{:S(2)}, u32[]{:S(2)}) collective-permute-start(bf16[64,32,128]{2,1,0:T(8,128)(2,1)S(1)} %all-to-all-done), channel_id=1, source_target_pairs={{0,1},{1,0},{2,3},{3,2},{4,5},{5,4},{6,7},{7,6},{8,9},{9,8},{10,11... | collective-permute-start | bytes 1572872 | tf_op jit(solution)/shard_map/ppermute | solution.py:393
